TPU v7x, 32 devices: a whole 2x2x4 slice. The times are simulated.
32 devices in a mesh: top: 4 (over x, core), low: 8 (over z, y).
Axes of the slice: x: 2, y: 2, z: 4, core: 2. Of those that a mesh axis runs over, the one named last changes fastest.
Arguments:
- segments: float32 [8192, 9, 128], P(('top', 'low')), may hold values from -1 to 1
- send_counts: int32 [32, 32], P(('top', 'low')), may hold values from 0 to 16, as said below
- send_offsets: int32 [32, 32], P(('top', 'low')), may hold values from 0 to 256, as said below
- leaf_of_block: int32 [8192], P(('top', 'low')), may hold values from 0 to 127
Outputs:
- leaf_moments: float32 [315, 4096], P(None, ('top', 'low'))
- root_moments: float32 [32, 315], P(('top', 'low'))
Inputs may be any that keep to these rules, and one draw needn't show every extreme that they name: `send_counts`: each row sums to 256; one owner, drawn from the seed, receives exactly 16 blocks from every domain. `send_offsets`: each row is the exclusive prefix sum of the same row of send_counts.
All inputs are finite; a program needn't handle non-finite values.
Results may differ from a plain program's by a relative error of at most 0.00017.
Values sent between devices are 32-bit elements; how exact they have to be, the bound alone decides.
A program may use at most 192 MiB of HBM per device.

v0:
```python
import math

import jax
import jax.numpy as jnp
import numpy as np
from jax import lax
from jax.sharding import PartitionSpec as P

MONOS = 35
COEFFS = 315
LEAF_DEV = 128


def swapped(block, axis, stride):
    count = lax.axis_size(axis)
    route = []
    for low in range(count):
        high = low | 1 << stride
        if high != low and high < count:
            route += [(low, high), (high, low)]
    return lax.ppermute(block, axis, route)


def make_exponents():
    collected = []
    for degree_total in range(5):
        for first_power in range(degree_total, -1, -1):
            for second_power in range(degree_total - first_power, -1, -1):
                collected.append(
                    (first_power, second_power, degree_total - first_power - second_power)
                )
    return np.array(collected, dtype=np.int32)


def make_shifts(which_axis):
    exponent_table = make_exponents()
    table = np.zeros((2, 35, 35), np.float32)
    for which_side in range(2):
        sign_value = -1.0 if which_side == 0 else 1.0
        for target_row in range(35):
            for source_col in range(35):
                target = exponent_table[target_row]
                source = exponent_table[source_col]
                agrees = all(
                    (target[other] == source[other] for other in range(3) if other != which_axis)
                )
                if agrees and source[which_axis] <= target[which_axis]:
                    upper_power = int(target[which_axis])
                    lower_power = int(source[which_axis])
                    table[which_side, target_row, source_col] = (
                        math.comb(upper_power, lower_power)
                        * sign_value ** (upper_power - lower_power)
                        * 0.5**upper_power
                    )
    return table


def quadrature():
    return ((-math.sqrt(0.6), 0.0, math.sqrt(0.6)), (5.0 / 18.0, 8.0 / 18.0, 5.0 / 18.0))


def block_moments(blocks):
    exponent_table = make_exponents()
    gauss_points, gauss_weights = quadrature()
    how_many = blocks.shape[0]
    seg_width = blocks.shape[2]
    burgers = blocks[:, 0:3]
    middle = blocks[:, 3:6]
    half_vector = blocks[:, 6:9]
    tensor = (burgers[:, :, None, :] * (2.0 * half_vector)[:, None, :, :]).reshape(
        how_many, 9, seg_width
    )
    monomials = jnp.zeros((how_many, 35, seg_width), jnp.float32)
    for gauss_point, weight in zip(gauss_points, gauss_weights):
        position = middle + gauss_point * half_vector
        squared = position * position
        powers = jnp.stack(
            [jnp.ones_like(position), position, squared, squared * position, squared * squared],
            axis=1,
        )
        monomials = monomials + weight * (
            powers[:, exponent_table[:, 0], 0]
            * powers[:, exponent_table[:, 1], 1]
            * powers[:, exponent_table[:, 2], 2]
        )
    moments = jnp.einsum("bas,bms->bam", tensor, monomials, precision=lax.Precision.HIGHEST)
    return (moments * seg_width ** (-0.5)).reshape(how_many, 9 * 35)


def combine_level(lower, upper, which_dim):
    tables = jnp.asarray(make_shifts(which_dim))
    left_part = jnp.einsum("mk,akn->amn", tables[0], lower, precision=lax.Precision.HIGHEST)
    right_part = jnp.einsum("mk,akn->amn", tables[1], upper, precision=lax.Precision.HIGHEST)
    return (left_part + right_part) * (1.0 / math.sqrt(2.0))


def reduce_tree(cells, first_level):
    levels = cells.shape[2].bit_length() - 1
    for level_index in range(levels):
        paired = cells.reshape(9, 35, -1, 2)
        cells = combine_level(paired[..., 0], paired[..., 1], (first_level + level_index) % 3)
    return cells


def local(segments, send_counts, send_offsets, leaf_of_block):
    counts_row = send_counts[0]
    offsets_row = send_offsets[0]
    owners_all = counts_row.shape[0]
    blocks_here = segments.shape[0]
    slot_limit = max(2, 2 * blocks_here // owners_all)
    seg_width = segments.shape[2]
    slot_ids = lax.iota(jnp.int32, slot_limit)
    is_live = slot_ids[None, :] < counts_row[:, None]
    chosen = jnp.where(is_live, offsets_row[:, None] + slot_ids[None, :], 0).reshape(-1)
    live_flat = is_live.reshape(-1)
    leaf_slots = jnp.where(live_flat, leaf_of_block[chosen], 0).reshape(owners_all, slot_limit)
    packed = jnp.where(live_flat[:, None, None], segments[chosen], 0.0).reshape(
        owners_all, slot_limit, 9, seg_width
    )
    blocks_in = lax.all_to_all(packed, ("top", "low"), split_axis=0, concat_axis=0, tiled=True)
    leaves_in = lax.all_to_all(leaf_slots, ("top", "low"), split_axis=0, concat_axis=0, tiled=True)
    sources = blocks_in.shape[0]
    slot_count = blocks_in.shape[1]
    result = block_moments(blocks_in.reshape(sources * slot_count, 9, seg_width)).reshape(
        sources, slot_count, COEFFS
    )
    selector = (leaves_in.reshape(-1)[:, None] == lax.iota(jnp.int32, LEAF_DEV)[None, :]).astype(
        jnp.float32
    )
    leaf_moments = lax.dot_general(
        result.reshape(-1, COEFFS),
        selector,
        (((0,), (0,)), ((), ())),
        precision=lax.Precision.HIGHEST,
    )
    local_levels = LEAF_DEV.bit_length() - 1
    cell = reduce_tree(leaf_moments.reshape(9, MONOS, LEAF_DEV), 0)
    low_bits = lax.axis_size("low").bit_length() - 1
    top_bits = lax.axis_size("top").bit_length() - 1
    low_index = lax.axis_index("low")
    for bit_number in range(low_bits):
        partner = swapped(cell, "low", bit_number)
        upper_side = low_index >> bit_number & 1 == 1
        lower_cell = jnp.where(upper_side, partner, cell)
        upper_cell = jnp.where(upper_side, cell, partner)
        cell = combine_level(lower_cell, upper_cell, (local_levels + bit_number) % 3)
    top_index = lax.axis_index("top")
    for bit_number in range(top_bits):
        partner = swapped(cell, "top", bit_number)
        upper_side = top_index >> bit_number & 1 == 1
        lower_cell = jnp.where(upper_side, partner, cell)
        upper_cell = jnp.where(upper_side, cell, partner)
        cell = combine_level(lower_cell, upper_cell, (local_levels + low_bits + bit_number) % 3)
    return (leaf_moments, cell.reshape(1, COEFFS))


def solution(mesh):
    placed = (
        P(("top", "low"), None, None),
        P(("top", "low"), None),
        P(("top", "low"), None),
        P(("top", "low")),
    )
    return jax.shard_map(
        local,
        mesh=mesh,
        in_specs=placed,
        out_specs=(P(None, ("top", "low")), P(("top", "low"), None)),
        check_vma=False,
    )
```

profile of v0, /device:TPU:0, one launch (start us, length us, event | category | flops | bytes accessed | tf_op | source)
XLA Modules:
  0.0 271.8 jit_solution(13298465278345092977)
XLA Ops:
  0.6 0.8 add_select_fusion
  1.6 0.6 copy-done.19
  2.2 3.6 %gather_fusion.10 = s32[512]{0:T(512)S(1)} fusion(s32[256]{0:T(256)} %param.37, s32[1024]{0:T(1024)S(1)} %pad_clamp_fusion), kind=kCustom, calls=%fused_computation.10 | custom fusion | bytes 6144 | tf_op jit(solution)/shard_map/gather | solution.py:116
  5.9 1.3 fusion.50
  7.2 7.3 %all-to-all-start.1 = ((s32[32,1,16]{2,1,0:T(1,128)}), s32[32,1,16]{2,1,0:T(1,128)S(1)}, u32[]{:S(2)}, u32[]{:S(2)}) async-start(s32[32,1,16]{2,1,0:T(1,128)} %bitcast.19), calls=%async_computation.1 | async-start | bytes 32768 | tf_op jit(solution)/shard_map/all_to_all | solution.py:121
  14.5 1.3 iota_compare_fusion.3
  15.9 5.4 %gather_fusion = f32[512,9,128]{2,0,1:T(8,128)S(1)} fusion(f32[256,9,128]{2,0,1:T(8,128)S(1)} %copy-done, s32[1024]{0:T(1024)} %copy-done.19), kind=kCustom, calls=%fused_computation | custom fusion | bytes 4720640 | tf_op jit(solution)/shard_map/gather | solution.py:117
  21.2 2.3 copy_select_fusion
  23.5 6.1 %all-to-all-start = ((f32[32,16,9,128]{3,1,2,0:T(8,128)}), f32[32,16,9,128]{3,1,2,0:T(8,128)}, u32[]{:S(2)}, u32[]{:S(2)}) async-start(f32[32,16,9,128]{3,1,2,0:T(8,128)} %copy_select_fusion), calls=%async_computation | async-start | bytes 4718592 | tf_op jit(solution)/shard_map/all_to_all | solution.py:120
  29.6 0.9 broadcast_dynamic-update-slice_fusion
  30.6 0.9 broadcast_dynamic-update-slice_fusion.1
  31.5 0.9 broadcast_dynamic-update-slice_fusion.2
  32.5 0.5 broadcast.274
  33.0 0.7 reduce.3
  33.7 51.6 %all-to-all-done = f32[32,16,9,128]{3,1,2,0:T(8,128)} async-done(((f32[32,16,9,128]{3,1,2,0:T(8,128)}), f32[32,16,9,128]{3,1,2,0:T(8,128)}, u32[]{:S(2)}, u32[]{:S(2)}) %all-to-all-start) | async-done | bytes 2359328 | tf_op jit(solution)/shard_map/all_to_all | solution.py:120
  85.4 1.9 copy.68
  87.3 1.5 bitcast_dynamic-update-slice_fusion.2
  88.8 0.9 copy-done.2
  89.7 1.2 fusion.27
  90.9 0.9 fusion.29
  91.9 1.0 fusion.31
  92.8 9.3 %gather_fusion.1 = f32[35,512,128]{2,1,0:T(8,128)} fusion(f32[512,5,3,128]{3,0,2,1:T(8,128)} %fusion.31, s32[35]{0:T(128)S(1)} %copy-done.5), kind=kCustom, calls=%fused_computation.1 | custom fusion | bytes 18350360 | tf_op jit(solution)/shard_map/gather | solution.py:82
  102.1 9.5 %gather_fusion.2 = f32[35,512,128]{2,1,0:T(8,128)} fusion(f32[512,5,3,128]{3,0,2,1:T(8,128)} %fusion.31, s32[35]{0:T(128)S(1)} %copy-done.4), kind=kCustom, calls=%fused_computation.2 | custom fusion | bytes 18350360 | tf_op jit(solution)/shard_map/gather | solution.py:83
  111.6 2.1 fusion.34
  113.7 2.1 fusion.36
  115.8 9.2 %gather_fusion.4 = f32[35,512,128]{2,1,0:T(8,128)} fusion(f32[512,5,3,128]{3,0,2,1:T(8,128)} %fusion.36, s32[35]{0:T(128)S(1)} %copy-done.5), kind=kCustom, calls=%fused_computation.4 | custom fusion | bytes 18350360 | tf_op jit(solution)/shard_map/gather | solution.py:82
  125.0 9.4 %gather_fusion.5 = f32[35,512,128]{2,1,0:T(8,128)} fusion(f32[512,5,3,128]{3,0,2,1:T(8,128)} %fusion.36, s32[35]{0:T(128)S(1)} %copy-done.4), kind=kCustom, calls=%fused_computation.5 | custom fusion | bytes 18350360 | tf_op jit(solution)/shard_map/gather | solution.py:83
  134.4 9.6 %gather_fusion.3 = f32[35,512,128]{2,1,0:T(8,128)} fusion(f32[512,5,3,128]{3,0,2,1:T(8,128)} %fusion.31, s32[35]{0:T(128)S(1)} %copy-done.3), kind=kCustom, calls=%fused_computation.3 | custom fusion | bytes 18350360 | tf_op jit(solution)/shard_map/gather | solution.py:84
  144.0 9.7 %gather_fusion.6 = f32[35,512,128]{2,1,0:T(8,128)} fusion(f32[512,5,3,128]{3,0,2,1:T(8,128)} %fusion.36, s32[35]{0:T(128)S(1)} %copy-done.3), kind=kCustom, calls=%fused_computation.6 | custom fusion | bytes 18350360 | tf_op jit(solution)/shard_map/gather | solution.py:84
  153.7 1.0 fusion.37
  154.7 1.0 fusion.39
  155.6 1.0 fusion.41
  156.6 9.2 %gather_fusion.7 = f32[35,512,128]{2,1,0:T(8,128)} fusion(f32[512,5,3,128]{3,0,2,1:T(8,128)} %fusion.41, s32[35]{0:T(128)S(1)} %copy-done.5), kind=kCustom, calls=%fused_computation.7 | custom fusion | bytes 18350360 | tf_op jit(solution)/shard_map/gather | solution.py:82
  165.8 9.6 %gather_fusion.8 = f32[35,512,128]{2,1,0:T(8,128)} fusion(f32[512,5,3,128]{3,0,2,1:T(8,128)} %fusion.41, s32[35]{0:T(128)S(1)} %copy-done.4), kind=kCustom, calls=%fused_computation.8 | custom fusion | bytes 18350360 | tf_op jit(solution)/shard_map/gather | solution.py:83
  175.4 9.5 %gather_fusion.9 = f32[35,512,128]{2,1,0:T(8,128)} fusion(f32[512,5,3,128]{3,0,2,1:T(8,128)} %fusion.41, s32[35]{0:T(128)S(1)} %copy-done.3), kind=kCustom, calls=%fused_computation.9 | custom fusion | bytes 18350360 | tf_op jit(solution)/shard_map/gather | solution.py:84
  185.1 1.6 broadcast_multiply_fusion
  186.7 27.5 %add_bitcast_fusion = f32[512,35,128]{2,0,1:T(8,128)S(1)} fusion(f32[35,512,128]{2,1,0:T(8,128)} %gather_fusion.9, f32[35,512,128]{2,1,0:T(8,128)} %gather_fusion.6, f32[35,512,128]{2,1,0:T(8,128)} %gather_fusion.3, f32[35,512,128]{2,1,0:T(8,128)} %gather_fusion.7, f32[35,512,128]{2,1,0:T(8,128)} %gather_fusion.8, f32[35,512,128]{2,1,0:T(8,128)} %gather_fusion.4, ...), kind=kLoop, calls=%fused_computation.13 | loop fusion | flops 25231360 | bytes 91750400 | tf_op jit(solution)/shard_map/add | solution.py:81
  214.2 27.6 %fusion.3 = f32[512,9,35]{2,1,0:T(8,128)} fusion(f32[512,35,128]{2,0,1:T(8,128)S(1)} %add_bitcast_fusion, f32[512,9,128]{2,0,1:T(8,128)} %bitcast.198), kind=kOutput, calls=%fused_computation.16 | convolution fusion | flops 247887360 | bytes 12179456 | tf_op jit(solution)/shard_map/bas,bms->bam/dot_general | solution.py:86
  241.8 3.4 %reshape.333 = f32[512,315]{1,0:T(8,128)S(1)} reshape(f32[512,9,35]{2,1,0:T(8,128)} %fusion.3) | data formatting | bytes 1290240 | tf_op jit(solution)/shard_map/reshape;reshape;reshape | solution.py:131
  245.3 0.9 fusion.42
  246.3 0.4 reshape_reshape.3
  246.9 0.2 copy.88
  247.1 0.2 copy.89
  247.3 0.3 fusion.44
  247.7 0.3 fusion.9
  248.0 0.2 copy.76
  248.2 0.3 fusion.89
  248.5 0.3 fusion.92
  248.8 0.3 fusion.10
  249.2 0.9 fusion.93
  250.1 0.9 fusion.11
  251.1 0.2 fusion.47
  251.3 0.2 fusion.12
  251.5 0.2 fusion.48
  251.7 0.2 fusion.13
  252.1 0.2 fusion.15
  252.6 3.6 %collective-permute-done = f32[9,35,1]{1,0,2:T(8,128)S(1)} collective-permute-done((f32[9,35,1]{1,0,2:T(8,128)S(1)}, f32[9,35,1]{1,0,2:T(8,128)S(1)}, u32[]{:S(2)}, u32[]{:S(2)}) %collective-permute-start) | collective-permute-done | bytes 1292 | tf_op jit(solution)/shard_map/ppermute | solution.py:21
  256.6 3.6 %collective-permute-done.1 = f32[9,35,1]{1,0,2:T(8,128)S(1)} collective-permute-done((f32[9,35,1]{1,0,2:T(8,128)S(1)}, f32[9,35,1]{1,0,2:T(8,128)S(1)}, u32[]{:S(2)}, u32[]{:S(2)}) %collective-permute-start.1) | collective-permute-done | bytes 1292 | tf_op jit(solution)/shard_map/ppermute | solution.py:21
  260.6 4.5 %collective-permute-done.2 = f32[9,35,1]{1,0,2:T(8,128)S(1)} collective-permute-done((f32[9,35,1]{1,0,2:T(8,128)S(1)}, f32[9,35,1]{1,0,2:T(8,128)S(1)}, u32[]{:S(2)}, u32[]{:S(2)}) %collective-permute-start.2) | collective-permute-done | bytes 1292 | tf_op jit(solution)/shard_map/ppermute | solution.py:21
  265.5 1.2 collective-permute-done.3
  266.8 0.2 fusion.18
  267.0 0.6 collective-permute-start.4
  267.5 3.1 %collective-permute-done.4 = f32[9,35,1]{1,0,2:T(8,128)S(1)} collective-permute-done((f32[9,35,1]{1,0,2:T(8,128)S(1)}, f32[9,35,1]{1,0,2:T(8,128)S(1)}, u32[]{:S(2)}, u32[]{:S(2)}) %collective-permute-start.4) | collective-permute-done | bytes 1292 | tf_op jit(solution)/shard_map/ppermute | solution.py:21
  271.0 0.7 reshape.256
  (65 shorter events, 2.8 us)
Async XLA Ops:
  0.6 15.2 %copy-start = (f32[256,9,128]{2,0,1:T(8,128)S(1)}, f32[256,9,128]{2,0,1:T(8,128)}, u32[]{:S(2)}) copy-start(f32[256,9,128]{2,0,1:T(8,128)} %param.34) | copy-start | bytes 3538948
  1.6 0.6 copy-start.19
  7.2 16.3 %all-to-all-start.1 = ((s32[32,1,16]{2,1,0:T(1,128)}), s32[32,1,16]{2,1,0:T(1,128)S(1)}, u32[]{:S(2)}, u32[]{:S(2)}) async-start(s32[32,1,16]{2,1,0:T(1,128)} %bitcast.19), calls=%async_computation.1 | async-start | bytes 32768 | tf_op jit(solution)/shard_map/all_to_all | solution.py:121
  23.5 61.9 %all-to-all-start = ((f32[32,16,9,128]{3,1,2,0:T(8,128)}), f32[32,16,9,128]{3,1,2,0:T(8,128)}, u32[]{:S(2)}, u32[]{:S(2)}) async-start(f32[32,16,9,128]{3,1,2,0:T(8,128)} %copy_select_fusion), calls=%async_computation | async-start | bytes 4718592 | tf_op jit(solution)/shard_map/all_to_all | solution.py:120
  88.8 0.9 copy-start.2
  88.8 4.0 %copy-start.5 = (s32[35]{0:T(128)S(1)}, s32[35]{0:T(128)}, u32[]{:S(2)}) copy-start(s32[35]{0:T(128)} %constant.230) | copy-start | bytes 424
  92.8 9.3 %copy-start.4 = (s32[35]{0:T(128)S(1)}, s32[35]{0:T(128)}, u32[]{:S(2)}) copy-start(s32[35]{0:T(128)} %constant.238) | copy-start | bytes 424
  125.0 9.4 %copy-start.3 = (s32[35]{0:T(128)S(1)}, s32[35]{0:T(128)}, u32[]{:S(2)}) copy-start(s32[35]{0:T(128)} %constant.246) | copy-start | bytes 424
  245.3 2.1 copy-start.7
  245.3 2.4 copy-start.10
  245.3 3.2 %copy-start.8 = (f32[35,35,1]{1,0,2:T(8,128)S(1)}, f32[35,35,1]{1,0,2:T(8,128)}, u32[]{:S(2)}) copy-start(f32[35,35,1]{1,0,2:T(8,128)} %constant.297) | copy-start | bytes 14704
  246.2 2.9 %copy-start.6 = (f32[315,128]{1,0:T(8,128)}, f32[315,128]{1,0:T(8,128)S(1)}, u32[]{:S(2)}) copy-start(f32[315,128]{1,0:T(8,128)S(1)} %fusion.42) | copy-start | bytes 483844
  246.2 2.6 copy-start.9
  246.3 25.3 %copy-start.1 = (f32[256,9,128]{2,0,1:T(8,128)S(1)}, f32[256,9,128]{2,0,1:T(8,128)}, u32[]{:S(2)}) copy-start(f32[256,9,128]{2,0,1:T(8,128)} %param.34) | copy-start | bytes 3538948
  246.7 13.7 %copy-start.11 = (f32[35,35]{1,0:T(8,128)S(1)}, f32[35,35]{1,0:T(8,128)}, u32[]{:S(2)}) copy-start(f32[35,35]{1,0:T(8,128)} %constant.103) | copy-start | bytes 14704
  246.8 5.1 %copy-start.17 = (f32[35,35,1]{1,0,2:T(8,128)S(1)}, f32[35,35,1]{1,0,2:T(8,128)}, u32[]{:S(2)}) copy-start(f32[35,35,1]{1,0,2:T(8,128)} %constant.299) | copy-start | bytes 14704
  246.9 5.2 %copy-start.18 = (f32[35,35,1]{1,0,2:T(8,128)S(1)}, f32[35,35,1]{1,0,2:T(8,128)}, u32[]{:S(2)}) copy-start(f32[35,35,1]{1,0,2:T(8,128)} %constant.300) | copy-start | bytes 14704
  246.9 5.4 %copy-start.15 = (f32[35,35]{1,0:T(8,128)S(1)}, f32[35,35]{1,0:T(8,128)}, u32[]{:S(2)}) copy-start(f32[35,35]{1,0:T(8,128)} %constant.95) | copy-start | bytes 14704
  246.9 5.5 %copy-start.16 = (f32[35,35]{1,0:T(8,128)S(1)}, f32[35,35]{1,0:T(8,128)}, u32[]{:S(2)}) copy-start(f32[35,35]{1,0:T(8,128)} %constant.97) | copy-start | bytes 14704
  246.9 9.4 %copy-start.14 = (f32[35,35]{1,0:T(8,128)S(1)}, f32[35,35]{1,0:T(8,128)}, u32[]{:S(2)}) copy-start(f32[35,35]{1,0:T(8,128)} %constant.101) | copy-start | bytes 14704
  246.9 9.5 %copy-start.13 = (f32[35,35]{1,0:T(8,128)S(1)}, f32[35,35]{1,0:T(8,128)}, u32[]{:S(2)}) copy-start(f32[35,35]{1,0:T(8,128)} %constant.99) | copy-start | bytes 14704
  246.9 13.3 %copy-start.12 = (f32[35,35]{1,0:T(8,128)S(1)}, f32[35,35]{1,0:T(8,128)}, u32[]{:S(2)}) copy-start(f32[35,35]{1,0:T(8,128)} %constant.105) | copy-start | bytes 14704
  252.6 3.7 %collective-permute-start = (f32[9,35,1]{1,0,2:T(8,128)S(1)}, f32[9,35,1]{1,0,2:T(8,128)S(1)}, u32[]{:S(2)}, u32[]{:S(2)}) collective-permute-start(f32[9,35,1]{1,0,2:T(8,128)S(1)} %fusion.26), channel_id=1, source_target_pairs={{0,1},{1,0},{2,3},{3,2},{4,5},{5,4},{6,7},{7,6},{8,9},{9,8},{10,11... | collective-permute-start | bytes 3788 | tf_op jit(solution)/shard_map/ppermute | solution.py:21
  256.6 3.7 %collective-permute-start.1 = (f32[9,35,1]{1,0,2:T(8,128)S(1)}, f32[9,35,1]{1,0,2:T(8,128)S(1)}, u32[]{:S(2)}, u32[]{:S(2)}) collective-permute-start(f32[9,35,1]{1,0,2:T(8,128)S(1)} %fusion.24), channel_id=1, source_target_pairs={{0,2},{2,0},{1,3},{3,1},{4,6},{6,4},{5,7},{7,5},{8,10},{10,8},{9,1... | collective-permute-start | bytes 3788 | tf_op jit(solution)/shard_map/ppermute | solution.py:21
  260.6 4.6 %collective-permute-start.2 = (f32[9,35,1]{1,0,2:T(8,128)S(1)}, f32[9,35,1]{1,0,2:T(8,128)S(1)}, u32[]{:S(2)}, u32[]{:S(2)}) collective-permute-start(f32[9,35,1]{1,0,2:T(8,128)S(1)} %fusion.22), channel_id=1, source_target_pairs={{0,4},{4,0},{1,5},{5,1},{2,6},{6,2},{3,7},{7,3},{8,12},{12,8},{9,1... | collective-permute-start | bytes 3788 | tf_op jit(solution)/shard_map/ppermute | solution.py:21
  265.4 1.2 collective-permute-start.3
  267.0 3.7 %collective-permute-start.4 = (f32[9,35,1]{1,0,2:T(8,128)S(1)}, f32[9,35,1]{1,0,2:T(8,128)S(1)}, u32[]{:S(2)}, u32[]{:S(2)}) collective-permute-start(f32[9,35,1]{1,0,2:T(8,128)S(1)} %fusion.18), channel_id=1, source_target_pairs={{0,16},{16,0},{8,24},{24,8},{1,17},{17,1},{9,25},{25,9},{2,18},{18... | collective-permute-start | bytes 3788 | tf_op jit(solution)/shard_map/ppermute | solution.py:21
where the time goes:
time: 276 us; the launch traced here: 272 us
  local copies, waits for them, and re-layouts  107 us (39%)
  waiting for transfers between devices  67.7 us (25%)
  other arithmetic  47.4 us (17%)
  matrix products  34.3 us (12%)
  starting transfers between devices  14.2 us (5%)
    all_to_all x1, waiting for transfers between devices, local(): lax.all_to_all(packed, ('top', 'low'), split_axis=0, concat_axis=0, tiled...  51.6 us
    gather x3, local copies, waits for them, and re-layouts, block_moments(): powers[:, exponent_table[:, 2], 2]  28.9 us
    gather x3, local copies, waits for them, and re-layouts, block_moments(): powers[:, exponent_table[:, 1], 1]  28.5 us
    gather x3, local copies, waits for them, and re-layouts, block_moments(): powers[:, exponent_table[:, 0], 0] * powers[:, exponent_table[:, 1], 1]  27.7 us
    dot_general x1, matrix products, block_moments(): jnp.einsum('bas,bms->bam', tensor, monomials, precision=lax.Precision.HIG...  27.6 us
    add x1, other arithmetic, block_moments(): monomials + weight * (powers[:, exponent_table[:, 0], 0] * powers[:, expo...  27.5 us
    ppermute x5, waiting for transfers between devices, swapped(): return lax.ppermute(block, axis, route)  16.1 us
    unnamed x6, other arithmetic  7.7 us
  transfers between devices with their start and end apart: 7, of which 6 were waited for; matrix products, arithmetic and copies ran while one was open for 5% of the time, Pallas kernels for 0%

commit v1 on v0

v1 whole, which is shorter than its diff:
```python
import functools
import math

import jax
import jax.numpy as jnp
import numpy as np
from jax import lax
from jax.experimental import pallas as pl
from jax.experimental.pallas import tpu as pltpu
from jax.sharding import PartitionSpec as P

MONOS = 35
COEFFS = 315
LEAF_DEV = 128
SLOTS = 16
ROWS = 2 * SLOTS + SLOTS // 2
MESH = pl.DeviceIdType.MESH
BF16 = jnp.bfloat16
F32 = jnp.float32
NT = (((1,), (1,)), ((), ()))
NN = (((1,), (0,)), ((), ()))


def make_exponents():
    collected = []
    for degree_total in range(5):
        for first_power in range(degree_total, -1, -1):
            for second_power in range(degree_total - first_power, -1, -1):
                collected.append(
                    (first_power, second_power, degree_total - first_power - second_power)
                )
    return collected


EXPONENTS = make_exponents()
POINTS = (
    (-math.sqrt(0.6), 5.0 / 18.0),
    (0.0, 8.0 / 18.0),
    (math.sqrt(0.6), 5.0 / 18.0),
)


def make_permutation():
    table = np.zeros((320, 384), np.float32)
    for m in range(MONOS):
        for a in range(9):
            table[MONOS * a + m, 128 * (m // 14) + 9 * (m % 14) + a] = 1.0
    return table


def split(x):
    high = x.astype(BF16)
    low = (x - high.astype(F32)).astype(BF16)
    return high, low


def dot(a, b, dims):
    return lax.dot_general(a, b, dims, preferred_element_type=F32)


def monomials(middle, half):
    total = None
    for point, weight in POINTS:
        at = [m + point * h if point else m for m, h in zip(middle, half)]
        made = {(0, 0, 0): None}
        values = []
        for e in EXPONENTS[1:]:
            axis = next(i for i in range(3) if e[i] > 0)
            lower = tuple(p - (i == axis) for i, p in enumerate(e))
            before = made[lower]
            made[e] = at[axis] * weight if before is None else before * at[axis]
            values.append(made[e])
        total = values if total is None else [x + y for x, y in zip(total, values)]
    return [jnp.ones_like(middle[0])] + total


def pair_products(quads, tensors):
    q_high, q_low = split(jnp.concatenate(quads, axis=0))
    t_high, t_low = split(jnp.concatenate(tensors + [jnp.zeros((56, 128), F32)], axis=0))
    left = jnp.concatenate([q_high, q_low], axis=1)
    right = jnp.concatenate([t_high, t_low], axis=0)
    both = dot(left, jnp.concatenate([right, right], axis=1), NT)
    return both[:, :128] + both[:, 128:]


def gather_same(products, spread):
    rows = products.shape[0]
    lane = lax.broadcasted_iota(jnp.int32, (rows, 128), 1)
    row = lax.broadcasted_iota(jnp.int32, (rows, 128), 0)
    kept = jnp.where(lax.rem(lane, 8) == lax.rem(row, 8), products, 0.0)
    high, low = split(kept)
    spreaded = dot(jnp.concatenate([high, low], axis=1), spread, NN)
    lane8 = lax.broadcasted_iota(jnp.int32, (8, 128), 1)
    tiles = []
    for first in (0, 14, 28):
        tile = jnp.zeros((8, 128), F32)
        for k in range(min(14, MONOS - first)):
            m = first + k
            here = (lane8 >= 9 * k) & (lane8 < 9 * k + 9)
            tile = jnp.where(here, spreaded[8 * m : 8 * m + 8], tile)
        tiles.append(tile)
    return tiles


def column(row):
    return jnp.transpose(jnp.broadcast_to(row, (128, 128)))


def kernel(
    devices, low_size, seg_ref, leaf_ref, perm_ref, spread_ref, count_ref, offset_ref,
    leaf_out, root_out,
    place, moments, acc, sbuf, rbuf, root_send, root_recv,
    send_sem, recv_sem, root_send_sem, root_recv_sem,
):
    me = lax.axis_index("top") * low_size + lax.axis_index("low")
    blocks = seg_ref.shape[1]
    groups = blocks // 8

    def partner(step):
        other = lax.rem(me + step, devices)
        return other, (other // low_size, lax.rem(other, low_size))

    barrier = pltpu.get_barrier_semaphore()

    def greet(step, carry):
        pl.semaphore_signal(barrier, inc=1, device_id=partner(step)[1], device_id_type=MESH)
        return carry

    lax.fori_loop(1, devices, greet, 0)

    leaves = leaf_ref[...]
    for chunk in range(blocks // 128):
        place[3, chunk * 128 : chunk * 128 + 128] = column(
            leaves[chunk : chunk + 1].astype(F32)
        )

    def load(group):
        rows = pl.ds(pl.multiple_of(group * 8, 8), 8)
        parts = [seg_ref[c, rows, :] for c in range(9)]
        scaled = [h * (2.0 / math.sqrt(128.0)) for h in parts[6:9]]
        tensors = [b * h for b in parts[0:3] for h in scaled]
        return rows, parts[3:6], parts[6:9], tensors

    lane8 = lax.broadcasted_iota(jnp.int32, (8, 128), 1)

    def p2m(group, carry):
        rows, middle, half, tensors = load(group)
        products = pair_products(monomials(middle, half), tensors)
        first, second, third = gather_same(products, spread_ref[...])
        moments[0, rows, :] = first
        moments[1, rows, :] = second
        moments[2, rows, :] = jnp.where(lane8 == 63, place[3, rows, :], third)
        return carry

    lax.fori_loop(0, groups, p2m, 0, unroll=2)
    for tile in range(3):
        moments[tile, blocks : blocks + SLOTS, :] = jnp.zeros((SLOTS, 128), F32)

    pl.semaphore_wait(barrier, devices - 1)

    lane16 = lax.broadcasted_iota(jnp.int32, (SLOTS, 128), 1)
    slot16 = lax.broadcasted_iota(jnp.int32, (SLOTS, 128), 0)

    def packed(owner):
        rows = pl.ds(offset_ref[0, owner], SLOTS)
        dead = (lane16 == 63) & (slot16 >= count_ref[0, owner])
        third = jnp.where(dead, -1.0, moments[2, rows, :])
        folded = jnp.where(lane8 < 64, third[:8], pltpu.roll(third[8:], 64, 1))
        return moments[0, rows, :], moments[1, rows, :], folded

    def put(ref, step, pieces):
        ref[step, 0:SLOTS, :] = pieces[0]
        ref[step, SLOTS : 2 * SLOTS, :] = pieces[1]
        ref[step, 2 * SLOTS : ROWS, :] = pieces[2]

    def block_copy(step):
        return pltpu.make_async_remote_copy(
            src_ref=sbuf.at[step], dst_ref=rbuf.at[step],
            send_sem=send_sem.at[step], recv_sem=recv_sem.at[step],
            device_id=partner(step)[1], device_id_type=MESH,
        )

    def root_copy(step):
        return pltpu.make_async_remote_copy(
            src_ref=root_send, dst_ref=root_recv.at[step],
            send_sem=root_send_sem.at[step], recv_sem=root_recv_sem.at[step],
            device_id=partner(step)[1], device_id_type=MESH,
        )

    def send_blocks(step, carry):
        put(sbuf, step, packed(partner(step)[0]))
        block_copy(step).start()
        return carry

    lax.fori_loop(1, devices, send_blocks, 0)
    put(rbuf, 0, packed(me))

    levels = LEAF_DEV.bit_length() - 1 + devices.bit_length() - 1
    depth = [len(range(d, levels, 3)) for d in range(3)]
    for chunk in range(blocks // 128):
        index = lax.broadcasted_iota(jnp.int32, (1, 128), 1) + chunk * 128
        owner = jnp.zeros((1, 128), jnp.int32)
        for o in range(devices):
            end = offset_ref[0, o] + count_ref[0, o]
            owner = owner + jnp.where(index >= end, 1, 0)
        cell = owner * LEAF_DEV + leaves[chunk : chunk + 1]
        for d in range(3):
            centre = jnp.zeros((1, 128), F32)
            for level in range(d, levels, 3):
                bit = lax.shift_right_logical(cell, level) & 1
                centre = centre + jnp.where(bit == 1, 1.0, -1.0) * 2.0 ** (level // 3)
            place[d, chunk * 128 : chunk * 128 + 128] = column(centre)

    acc[...] = jnp.zeros_like(acc)

    def to_root(group, carry):
        rows, middle, half, tensors = load(group)
        shrink = [0.5**k for k in depth]
        middle = [(p + place[d, rows, :]) * shrink[d] for d, p in enumerate(middle)]
        half = [h * shrink[d] for d, h in enumerate(half)]
        acc[...] += pair_products(monomials(middle, half), tensors)
        return carry

    lax.fori_loop(0, groups, to_root, 0, unroll=2)
    tiles = gather_same(acc[...] * 2.0 ** (-levels / 2), spread_ref[...])
    own = jnp.concatenate(
        [jnp.sum(t, axis=0, keepdims=True) for t in tiles] + [jnp.zeros((5, 128), F32)], axis=0
    )
    root_send[...] = own

    def send_root(step, carry):
        root_copy(step).start()
        return carry

    lax.fori_loop(1, devices, send_root, 0)

    def take(step, carry):
        block_copy(step).wait()
        return carry

    lax.fori_loop(1, devices, take, 0)

    half_rows = devices * 8
    flat = lambda x: x.reshape(half_rows, 128)
    near = [flat(rbuf[:, 0:8]), flat(rbuf[:, 16:24]), flat(rbuf[:, 32:40])]
    far = [flat(rbuf[:, 8:16]), flat(rbuf[:, 24:32]), pltpu.roll(near[2], 64, 1)]
    leaf_lane = lax.broadcasted_iota(jnp.int32, (half_rows, 128), 1).astype(F32)
    cells = jnp.zeros((LEAF_DEV, 384), F32)
    for side in (near, far):
        hit = jnp.where(side[2][:, 63:64] == leaf_lane, 1.0, 0.0)
        hit = jnp.transpose(hit).astype(BF16)
        high, low = split(jnp.concatenate(side, axis=1))
        cells = cells + dot(hit, high, NN) + dot(hit, low, NN)
    perm = perm_ref[...]
    high, low = split(cells)
    leaf_out[...] = (dot(perm, high, NT) + dot(perm, low, NT))[:COEFFS]

    def take_root(step, carry):
        root_copy(step).wait()
        return carry

    lax.fori_loop(1, devices, take_root, 0)
    root_recv[0] = own
    total = jnp.sum(root_recv[...], axis=0)
    line = jnp.concatenate([total[0:1], total[1:2], total[2:3]], axis=1)
    high, low = split(jnp.broadcast_to(line, (16, 384)))
    root_out[...] = (dot(high, perm, NT) + dot(low, perm, NT))[0:1, :COEFFS]


def local(devices, low_size, segments, send_counts, send_offsets, leaf_of_block):
    blocks = segments.shape[0]
    lanes = np.arange(128)
    one = ((lanes[None, :] % 9 == lanes[:, None] // 8) & (lanes[:, None] < 72)).astype(np.float32)
    spread = jnp.asarray(np.concatenate([one, one], axis=0), BF16)
    perm = jnp.asarray(make_permutation(), BF16)
    vmem = pl.BlockSpec(memory_space=pltpu.VMEM)
    smem = pl.BlockSpec(memory_space=pltpu.SMEM)
    dma = pltpu.SemaphoreType.DMA
    return pl.pallas_call(
        functools.partial(kernel, devices, low_size),
        out_shape=(
            jax.ShapeDtypeStruct((COEFFS, LEAF_DEV), F32),
            jax.ShapeDtypeStruct((1, COEFFS), F32),
        ),
        in_specs=[vmem, vmem, vmem, vmem, smem, smem],
        out_specs=(vmem, vmem),
        scratch_shapes=[
            pltpu.VMEM((4, blocks, 128), F32),
            pltpu.VMEM((3, blocks + SLOTS, 128), F32),
            pltpu.VMEM((8 * MONOS, 128), F32),
            pltpu.VMEM((devices, ROWS, 128), F32),
            pltpu.VMEM((devices, ROWS, 128), F32),
            pltpu.VMEM((8, 128), F32),
            pltpu.VMEM((devices, 8, 128), F32),
            dma((devices,)),
            dma((devices,)),
            dma((devices,)),
            dma((devices,)),
        ],
        compiler_params=pltpu.CompilerParams(
            collective_id=0, has_side_effects=True, vmem_limit_bytes=40 * 1024 * 1024
        ),
        cost_estimate=pl.CostEstimate(
            flops=2 * blocks * 128 * COEFFS * 2, bytes_accessed=blocks * 128 * 40, transcendentals=0
        ),
    )(
        jnp.transpose(segments, (1, 0, 2)),
        leaf_of_block.reshape(blocks // 128, 128),
        perm,
        spread,
        send_counts,
        send_offsets,
    )


def solution(mesh):
    placed = (
        P(("top", "low"), None, None),
        P(("top", "low"), None),
        P(("top", "low"), None),
        P(("top", "low")),
    )
    return jax.shard_map(
        functools.partial(local, mesh.size, mesh.shape["low"]),
        mesh=mesh,
        in_specs=placed,
        out_specs=(P(None, ("top", "low")), P(("top", "low"), None)),
        check_vma=False,
    )
```

time: 276 us -> 42.7 us (0.15); the launches traced: 272 us -> 42.4 us
  local copies, waits for them, and re-layouts: 107 us -> 6.26 us
  waiting for transfers between devices: 67.7 us -> 0 us
  other arithmetic: 47.4 us -> 0 us
  Pallas kernels: 0 us -> 35.5 us
  matrix products: 34.3 us -> 0 us
  starting transfers between devices: 14.2 us -> 0 us
    gather x12 -> x0, local copies, waits for them, and re-layouts: 94.1 us -> none  [the longest x3 28.9 us: block_moments(): powers[:, exponent_table[:, 2], 2]]
    all_to_all x2 -> x0, waiting for transfers between devices: 51.6 us -> none  [the longest x1 51.6 us: local(): lax.all_to_all(packed, ('top', 'low'), split_axis=0, concat_axis=0, tiled...]
    pallas_call x0 -> x1, Pallas kernels: none -> 35.5 us  [local(): pl.pallas_call(functools.partial(kernel, devices, low_size), out_shape=(j...]
    dot_general x26 -> x0, matrix products: 34.3 us -> none  [the longest x1 27.6 us: block_moments(): jnp.einsum('bas,bms->bam', tensor, monomials, precision=lax.Precision.HIG...]
    add x1 -> x0, other arithmetic: 27.5 us -> none  [block_moments(): monomials + weight * (powers[:, exponent_table[:, 0], 0] * powers[:, expo...]
    ppermute x5 -> x0, waiting for transfers between devices: 16.1 us -> none  [swapped(): return lax.ppermute(block, axis, route)]
    all_to_all x2 -> x0, starting transfers between devices: 13.4 us -> none  [the longest x1 7.3 us: local(): lax.all_to_all(leaf_slots, ('top', 'low'), split_axis=0, concat_axis=0, t...]
    unnamed x6 -> x0, other arithmetic: 7.7 us -> none
  transfers between devices with their start and end apart: 7 -> 0, of which waited for: 6 -> 0; matrix products, arithmetic and copies ran while one was open for 5% -> 0% of each run, Pallas kernels for 0% -> 0%
where the time goes in v1:
time: 42.7 us; the launch traced here: 42.4 us
  Pallas kernels  35.5 us (83%)
  local copies, waits for them, and re-layouts  6.26 us (15%)
  between operations  0.65 us (2%)
    pallas_call x1, Pallas kernels, local(): pl.pallas_call(functools.partial(kernel, devices, low_size), out_shape=(j...  35.5 us
    unnamed x14, local copies, waits for them, and re-layouts  6.26 us

profile of v1, /device:TPU:0, one launch (start us, length us, event | category | flops | bytes accessed | tf_op | source)
XLA Modules:
  0.0 42.4 jit_solution(4410508511776693844)
XLA Ops:
  0.6 0.0 copy-start
  0.6 1.3 %copy-done = f32[256,9,128]{2,0,1:T(8,128)S(1)} copy-done((f32[256,9,128]{2,0,1:T(8,128)S(1)}, f32[256,9,128]{2,0,1:T(8,128)}, u32[]{:S(2)}) %copy-start) | copy-done | bytes 1179672
  1.9 0.0 copy-start.1
  1.9 0.9 %copy-done.1 = bf16[320,384]{1,0:T(8,128)(2,1)S(1)} copy-done((bf16[320,384]{1,0:T(8,128)(2,1)S(1)}, bf16[320,384]{1,0:T(8,128)(2,1)}, u32[]{:S(2)}) %copy-start.1) | copy-done | bytes 245784
  2.8 0.0 copy-start.2
  2.8 0.8 %copy-done.2 = bf16[256,128]{1,0:T(8,128)(2,1)S(1)} copy-done((bf16[256,128]{1,0:T(8,128)(2,1)S(1)}, bf16[256,128]{1,0:T(8,128)(2,1)}, u32[]{:S(2)}) %copy-start.2) | copy-done | bytes 65560
  3.7 0.0 copy-start.3
  3.7 0.7 %copy-done.3 = s32[256]{0:T(256)S(1)} copy-done((s32[256]{0:T(256)S(1)}, s32[256]{0:T(256)}, u32[]{:S(2)}) %copy-start.3) | copy-done | bytes 1048
  4.4 0.0 copy-start.4
  4.4 0.7 %copy-done.4 = s32[1,32]{1,0:T(1,128)S(1)} copy-done((s32[1,32]{1,0:T(1,128)S(1)}, s32[1,32]{1,0:T(1,128)}, u32[]{:S(2)}) %copy-start.4) | copy-done | bytes 152
  5.0 0.0 copy-start.5
  5.0 0.7 %copy-done.5 = s32[1,32]{1,0:T(1,128)S(1)} copy-done((s32[1,32]{1,0:T(1,128)S(1)}, s32[1,32]{1,0:T(1,128)}, u32[]{:S(2)}) %copy-start.5) | copy-done | bytes 152
  5.7 35.5 %shard_map.77 = (f32[315,128]{1,0:T(8,128)S(1)}, f32[1,315]{1,0:T(1,128)S(1)}) custom-call(f32[9,256,128]{2,1,0:T(8,128)S(1)} %bitcast.2, s32[2,128]{1,0:T(2,128)S(1)} %bitcast.3, bf16[320,384]{1,0:T(8,128)(2,1)S(1)} %copy-done.1, bf16[256,128]{1,0:T(8,128)(2,1)S(1)} %copy-done.2, s32[1,32]{1,0:T(1,128)S(1)} %copy-done.4, s32[1,32]{1,0:T(1,128)S(1)} %copy-done.5), custom_call_target="tpu_custom_call" | custom-call | flops 41287680 | bytes 1310720 | tf_op jit(solution)/shard_map/pallas_call | solution.py:279
  41.2 0.7 %copy.10 = f32[315,128]{1,0:T(8,128)} copy(f32[315,128]{1,0:T(8,128)S(1)} %get-tuple-element.4) | data formatting | bytes 322560
  41.9 0.6 %copy.11 = f32[1,315]{1,0:T(1,128)} copy(f32[1,315]{1,0:T(1,128)S(1)} %get-tuple-element.5) | data formatting | bytes 2520
Async XLA Ops:
  0.6 1.3 %copy-start = (f32[256,9,128]{2,0,1:T(8,128)S(1)}, f32[256,9,128]{2,0,1:T(8,128)}, u32[]{:S(2)}) copy-start(f32[256,9,128]{2,0,1:T(8,128)} %param.6) | copy-start | bytes 3538948
  1.9 0.9 %copy-start.1 = (bf16[320,384]{1,0:T(8,128)(2,1)S(1)}, bf16[320,384]{1,0:T(8,128)(2,1)}, u32[]{:S(2)}) copy-start(bf16[320,384]{1,0:T(8,128)(2,1)} %constant.5.clone.perm_ref) | copy-start | bytes 737284
  2.8 0.8 %copy-start.2 = (bf16[256,128]{1,0:T(8,128)(2,1)S(1)}, bf16[256,128]{1,0:T(8,128)(2,1)}, u32[]{:S(2)}) copy-start(bf16[256,128]{1,0:T(8,128)(2,1)} %constant.4.clone.spread_ref) | copy-start | bytes 196612
  3.7 0.7 %copy-start.3 = (s32[256]{0:T(256)S(1)}, s32[256]{0:T(256)}, u32[]{:S(2)}) copy-start(s32[256]{0:T(256)} %param.9) | copy-start | bytes 3076
  4.4 0.7 %copy-start.4 = (s32[1,32]{1,0:T(1,128)S(1)}, s32[1,32]{1,0:T(1,128)}, u32[]{:S(2)}) copy-start(s32[1,32]{1,0:T(1,128)} %count_ref.1) | copy-start | bytes 388
  5.0 0.7 %copy-start.5 = (s32[1,32]{1,0:T(1,128)S(1)}, s32[1,32]{1,0:T(1,128)}, u32[]{:S(2)}) copy-start(s32[1,32]{1,0:T(1,128)} %offset_ref.1) | copy-start | bytes 388

commit v2 on v1

--- a/solution.py
+++ b/solution.py
@@ -14,6 +14,7 @@
 LEAF_DEV = 128
 SLOTS = 16
 ROWS = 2 * SLOTS + SLOTS // 2
+TOGETHER = 4
 MESH = pl.DeviceIdType.MESH
 BF16 = jnp.bfloat16
 F32 = jnp.float32
@@ -83,23 +84,24 @@
     return both[:, :128] + both[:, 128:]
 
 
-def gather_same(products, spread):
-    rows = products.shape[0]
-    lane = lax.broadcasted_iota(jnp.int32, (rows, 128), 1)
-    row = lax.broadcasted_iota(jnp.int32, (rows, 128), 0)
-    kept = jnp.where(lax.rem(lane, 8) == lax.rem(row, 8), products, 0.0)
-    high, low = split(kept)
-    spreaded = dot(jnp.concatenate([high, low], axis=1), spread, NN)
-    lane8 = lax.broadcasted_iota(jnp.int32, (8, 128), 1)
-    tiles = []
-    for first in (0, 14, 28):
-        tile = jnp.zeros((8, 128), F32)
-        for k in range(min(14, MONOS - first)):
-            m = first + k
-            here = (lane8 >= 9 * k) & (lane8 < 9 * k + 9)
-            tile = jnp.where(here, spreaded[8 * m : 8 * m + 8], tile)
-        tiles.append(tile)
-    return tiles
+def gather_same(products, same, spread, lane):
+    sides = []
+    for one in products:
+        kept = (one.reshape(MONOS, 8, 128) * same).reshape(8 * MONOS, 128)
+        sides.append(jnp.concatenate(split(kept), axis=1))
+    spreaded = dot(jnp.concatenate(sides, axis=0), spread, NN)
+    groups = []
+    for g in range(len(products)):
+        tiles = []
+        for first in (0, 14, 28):
+            count = min(14, MONOS - first)
+            tile = jnp.zeros((8, 128), F32)
+            for k in reversed(range(count)):
+                at = 8 * (MONOS * g + first + k)
+                tile = jnp.where(lane < 9 * k + 9, spreaded[at : at + 8], tile)
+            tiles.append(tile)
+        groups.append(tiles)
+    return groups
 
 
 def column(row):
@@ -107,14 +109,31 @@
 
 
 def kernel(
-    devices, low_size, seg_ref, leaf_ref, perm_ref, spread_ref, count_ref, offset_ref,
+    devices, low_size, cap,
+    seg_hbm, leaf_hbm, perm_hbm, spread_hbm, count_hbm, offset_hbm,
     leaf_out, root_out,
+    seg_ref, leaf_ref, perm_ref, spread_ref, count_ref, offset_ref,
     place, moments, acc, sbuf, rbuf, root_send, root_recv,
-    send_sem, recv_sem, root_send_sem, root_recv_sem,
+    load_sem, send_sem, recv_sem, root_send_sem, root_recv_sem,
 ):
+    fetches = [
+        pltpu.make_async_copy(src, dst, load_sem.at[i])
+        for i, (src, dst) in enumerate(
+            (
+                (leaf_hbm, leaf_ref),
+                (seg_hbm, seg_ref),
+                (spread_hbm, spread_ref),
+                (count_hbm, count_ref),
+                (offset_hbm, offset_ref),
+                (perm_hbm, perm_ref),
+            )
+        )
+    ]
+    for fetch in fetches:
+        fetch.start()
+
     me = lax.axis_index("top") * low_size + lax.axis_index("low")
     blocks = seg_ref.shape[1]
-    groups = blocks // 8
 
     def partner(step):
         other = lax.rem(me + step, devices)
@@ -127,12 +146,21 @@
         return carry
 
     lax.fori_loop(1, devices, greet, 0)
-
+    moments[...] = jnp.zeros_like(moments)
+    acc[...] = jnp.zeros_like(acc)
+
+    fetches[0].wait()
     leaves = leaf_ref[...]
     for chunk in range(blocks // 128):
         place[3, chunk * 128 : chunk * 128 + 128] = column(
             leaves[chunk : chunk + 1].astype(F32)
         )
+    for fetch in fetches[1:5]:
+        fetch.wait()
+
+    lane8 = lax.broadcasted_iota(jnp.int32, (8, 128), 1)
+    row8 = lax.broadcasted_iota(jnp.int32, (8, 128), 0)
+    same = jnp.where(lax.rem(lane8, 8) == row8, 1.0, 0.0)
 
     def load(group):
         rows = pl.ds(pl.multiple_of(group * 8, 8), 8)
@@ -141,22 +169,20 @@
         tensors = [b * h for b in parts[0:3] for h in scaled]
         return rows, parts[3:6], parts[6:9], tensors
 
-    lane8 = lax.broadcasted_iota(jnp.int32, (8, 128), 1)
-
-    def p2m(group, carry):
-        rows, middle, half, tensors = load(group)
-        products = pair_products(monomials(middle, half), tensors)
-        first, second, third = gather_same(products, spread_ref[...])
-        moments[0, rows, :] = first
-        moments[1, rows, :] = second
-        moments[2, rows, :] = jnp.where(lane8 == 63, place[3, rows, :], third)
-        return carry
-
-    lax.fori_loop(0, groups, p2m, 0, unroll=2)
-    for tile in range(3):
-        moments[tile, blocks : blocks + SLOTS, :] = jnp.zeros((SLOTS, 128), F32)
-
-    pl.semaphore_wait(barrier, devices - 1)
+    def p2m(first_group):
+        def body(turn, carry):
+            products, places = [], []
+            for u in range(TOGETHER):
+                rows, middle, half, tensors = load(first_group + turn * TOGETHER + u)
+                products.append(pair_products(monomials(middle, half), tensors))
+                places.append(rows)
+            for rows, tiles in zip(places, gather_same(products, same, spread_ref[...], lane8)):
+                moments[0, rows, :] = tiles[0]
+                moments[1, rows, :] = tiles[1]
+                moments[2, rows, :] = jnp.where(lane8 == 63, place[3, rows, :], tiles[2])
+            return carry
+
+        return body
 
     lane16 = lax.broadcasted_iota(jnp.int32, (SLOTS, 128), 1)
     slot16 = lax.broadcasted_iota(jnp.int32, (SLOTS, 128), 0)
@@ -187,12 +213,39 @@
             device_id=partner(step)[1], device_id_type=MESH,
         )
 
-    def send_blocks(step, carry):
-        put(sbuf, step, packed(partner(step)[0]))
-        block_copy(step).start()
-        return carry
-
-    lax.fori_loop(1, devices, send_blocks, 0)
+    quarter = blocks // 4
+    ready = quarter // cap
+    turns = quarter // (8 * TOGETHER)
+    lax.fori_loop(0, turns, p2m(0), 0)
+    lax.fori_loop(0, turns, p2m(3 * quarter // 8), 0)
+    pl.semaphore_wait(barrier, devices - 1)
+
+    def send_early(turn, carry):
+        spot = lax.rem(me + turn, 2 * ready)
+        owner = jnp.where(spot < ready, spot, devices - 2 * ready + spot)
+        step = lax.rem(owner - me + devices, devices)
+
+        @pl.when(step != 0)
+        def _():
+            put(sbuf, step, packed(owner))
+            block_copy(step).start()
+
+        return carry
+
+    lax.fori_loop(0, 2 * ready, send_early, 0)
+    lax.fori_loop(0, 2 * turns, p2m(quarter // 8), 0)
+
+    def send_late(step, carry):
+        owner = partner(step)[0]
+
+        @pl.when((owner >= ready) & (owner < devices - ready))
+        def _():
+            put(sbuf, step, packed(owner))
+            block_copy(step).start()
+
+        return carry
+
+    lax.fori_loop(1, devices, send_late, 0)
     put(rbuf, 0, packed(me))
 
     levels = LEAF_DEV.bit_length() - 1 + devices.bit_length() - 1
@@ -211,18 +264,20 @@
                 centre = centre + jnp.where(bit == 1, 1.0, -1.0) * 2.0 ** (level // 3)
             place[d, chunk * 128 : chunk * 128 + 128] = column(centre)
 
-    acc[...] = jnp.zeros_like(acc)
-
-    def to_root(group, carry):
-        rows, middle, half, tensors = load(group)
+    def to_root(turn, carry):
         shrink = [0.5**k for k in depth]
-        middle = [(p + place[d, rows, :]) * shrink[d] for d, p in enumerate(middle)]
-        half = [h * shrink[d] for d, h in enumerate(half)]
-        acc[...] += pair_products(monomials(middle, half), tensors)
-        return carry
-
-    lax.fori_loop(0, groups, to_root, 0, unroll=2)
-    tiles = gather_same(acc[...] * 2.0 ** (-levels / 2), spread_ref[...])
+        total = None
+        for u in range(2):
+            rows, middle, half, tensors = load(turn * 2 + u)
+            middle = [(p + place[d, rows, :]) * shrink[d] for d, p in enumerate(middle)]
+            half = [h * shrink[d] for d, h in enumerate(half)]
+            products = pair_products(monomials(middle, half), tensors)
+            total = products if total is None else total + products
+        acc[...] += total
+        return carry
+
+    lax.fori_loop(0, blocks // 16, to_root, 0)
+    (tiles,) = gather_same([acc[...] * 2.0 ** (-levels / 2)], same, spread_ref[...], lane8)
     own = jnp.concatenate(
         [jnp.sum(t, axis=0, keepdims=True) for t in tiles] + [jnp.zeros((5, 128), F32)], axis=0
     )
@@ -238,19 +293,22 @@
         block_copy(step).wait()
         return carry
 
-    lax.fori_loop(1, devices, take, 0)
-
-    half_rows = devices * 8
+    part = devices // 2
+    half_rows = part * 8
     flat = lambda x: x.reshape(half_rows, 128)
-    near = [flat(rbuf[:, 0:8]), flat(rbuf[:, 16:24]), flat(rbuf[:, 32:40])]
-    far = [flat(rbuf[:, 8:16]), flat(rbuf[:, 24:32]), pltpu.roll(near[2], 64, 1)]
     leaf_lane = lax.broadcasted_iota(jnp.int32, (half_rows, 128), 1).astype(F32)
     cells = jnp.zeros((LEAF_DEV, 384), F32)
-    for side in (near, far):
-        hit = jnp.where(side[2][:, 63:64] == leaf_lane, 1.0, 0.0)
-        hit = jnp.transpose(hit).astype(BF16)
-        high, low = split(jnp.concatenate(side, axis=1))
-        cells = cells + dot(hit, high, NN) + dot(hit, low, NN)
+    for start in (0, part):
+        lax.fori_loop(max(start, 1), start + part, take, 0)
+        got = pl.ds(start, part)
+        near = [flat(rbuf[got, 0:8]), flat(rbuf[got, 16:24]), flat(rbuf[got, 32:40])]
+        far = [flat(rbuf[got, 8:16]), flat(rbuf[got, 24:32]), pltpu.roll(near[2], 64, 1)]
+        for side in (near, far):
+            hit = jnp.where(side[2][:, 63:64] == leaf_lane, 1.0, 0.0)
+            hit = jnp.transpose(hit).astype(BF16)
+            high, low = split(jnp.concatenate(side, axis=1))
+            cells = cells + dot(hit, high, NN) + dot(hit, low, NN)
+    fetches[5].wait()
     perm = perm_ref[...]
     high, low = split(cells)
     leaf_out[...] = (dot(perm, high, NT) + dot(perm, low, NT))[:COEFFS]
@@ -274,17 +332,24 @@
     spread = jnp.asarray(np.concatenate([one, one], axis=0), BF16)
     perm = jnp.asarray(make_permutation(), BF16)
     vmem = pl.BlockSpec(memory_space=pltpu.VMEM)
-    smem = pl.BlockSpec(memory_space=pltpu.SMEM)
+    hbm = pl.BlockSpec(memory_space=pltpu.HBM)
+    cap = max(2, 2 * blocks // devices)
     dma = pltpu.SemaphoreType.DMA
     return pl.pallas_call(
-        functools.partial(kernel, devices, low_size),
+        functools.partial(kernel, devices, low_size, cap),
         out_shape=(
             jax.ShapeDtypeStruct((COEFFS, LEAF_DEV), F32),
             jax.ShapeDtypeStruct((1, COEFFS), F32),
         ),
-        in_specs=[vmem, vmem, vmem, vmem, smem, smem],
+        in_specs=[hbm] * 6,
         out_specs=(vmem, vmem),
         scratch_shapes=[
+            pltpu.VMEM((9, blocks, 128), F32),
+            pltpu.VMEM((blocks // 128, 128), jnp.int32),
+            pltpu.VMEM((320, 384), BF16),
+            pltpu.VMEM((256, 128), BF16),
+            pltpu.SMEM((1, devices), jnp.int32),
+            pltpu.SMEM((1, devices), jnp.int32),
             pltpu.VMEM((4, blocks, 128), F32),
             pltpu.VMEM((3, blocks + SLOTS, 128), F32),
             pltpu.VMEM((8 * MONOS, 128), F32),
@@ -292,6 +357,7 @@
             pltpu.VMEM((devices, ROWS, 128), F32),
             pltpu.VMEM((8, 128), F32),
             pltpu.VMEM((devices, 8, 128), F32),
+            dma((6,)),
             dma((devices,)),
             dma((devices,)),
             dma((devices,)),

time: 42.7 us -> 35.7 us (0.84)
  Pallas kernels: 35.5 us -> 28.5 us
    pallas_call x1, Pallas kernels: 35.5 us -> 28.5 us  [local(): pl.pallas_call(functools.partial(kernel, devices, low_size, cap), out_sha...]
where the time goes in v2:
time: 35.7 us; the launch traced here: 35.4 us
  Pallas kernels  28.5 us (80%)
  local copies, waits for them, and re-layouts  6.26 us (18%)
  between operations  0.65 us (2%)
    pallas_call x1, Pallas kernels, local(): pl.pallas_call(functools.partial(kernel, devices, low_size, cap), out_sha...  28.5 us
    unnamed x14, local copies, waits for them, and re-layouts  6.26 us

profile of v2, /device:TPU:0, one launch (start us, length us, event | category | flops | bytes accessed | tf_op | source)
XLA Modules:
  0.0 35.4 jit_solution(582537643739818795)
XLA Ops:
  0.6 0.0 copy-start
  0.6 1.3 %copy-done = f32[256,9,128]{2,0,1:T(8,128)S(1)} copy-done((f32[256,9,128]{2,0,1:T(8,128)S(1)}, f32[256,9,128]{2,0,1:T(8,128)}, u32[]{:S(2)}) %copy-start) | copy-done | bytes 1179672
  1.9 0.0 copy-start.1
  1.9 0.9 %copy-done.1 = bf16[320,384]{1,0:T(8,128)(2,1)S(1)} copy-done((bf16[320,384]{1,0:T(8,128)(2,1)S(1)}, bf16[320,384]{1,0:T(8,128)(2,1)}, u32[]{:S(2)}) %copy-start.1) | copy-done | bytes 245784
  2.8 0.0 copy-start.2
  2.8 0.8 %copy-done.2 = bf16[256,128]{1,0:T(8,128)(2,1)S(1)} copy-done((bf16[256,128]{1,0:T(8,128)(2,1)S(1)}, bf16[256,128]{1,0:T(8,128)(2,1)}, u32[]{:S(2)}) %copy-start.2) | copy-done | bytes 65560
  3.7 0.0 copy-start.3
  3.7 0.7 %copy-done.3 = s32[256]{0:T(256)S(1)} copy-done((s32[256]{0:T(256)S(1)}, s32[256]{0:T(256)}, u32[]{:S(2)}) %copy-start.3) | copy-done | bytes 1048
  4.4 0.0 copy-start.4
  4.4 0.7 %copy-done.4 = s32[1,32]{1,0:T(1,128)S(1)} copy-done((s32[1,32]{1,0:T(1,128)S(1)}, s32[1,32]{1,0:T(1,128)}, u32[]{:S(2)}) %copy-start.4) | copy-done | bytes 152
  5.0 0.0 copy-start.5
  5.0 0.7 %copy-done.5 = s32[1,32]{1,0:T(1,128)S(1)} copy-done((s32[1,32]{1,0:T(1,128)S(1)}, s32[1,32]{1,0:T(1,128)}, u32[]{:S(2)}) %copy-start.5) | copy-done | bytes 152
  5.7 28.5 %shard_map.77 = (f32[315,128]{1,0:T(8,128)S(1)}, f32[1,315]{1,0:T(1,128)S(1)}) custom-call(f32[9,256,128]{2,1,0:T(8,128)S(1)} %bitcast.2, s32[2,128]{1,0:T(2,128)S(1)} %bitcast.3, bf16[320,384]{1,0:T(8,128)(2,1)S(1)} %copy-done.1, bf16[256,128]{1,0:T(8,128)(2,1)S(1)} %copy-done.2, s32[1,32]{1,0:T(1,128)S(1)} %copy-done.4, s32[1,32]{1,0:T(1,128)S(1)} %copy-done.5), custom_call_target="tpu_custom_call" | custom-call | flops 41287680 | bytes 1310720 | tf_op jit(solution)/shard_map/pallas_call | solution.py:338
  34.2 0.7 %copy.10 = f32[315,128]{1,0:T(8,128)} copy(f32[315,128]{1,0:T(8,128)S(1)} %get-tuple-element.4) | data formatting | bytes 322560
  34.9 0.6 %copy.11 = f32[1,315]{1,0:T(1,128)} copy(f32[1,315]{1,0:T(1,128)S(1)} %get-tuple-element.5) | data formatting | bytes 2520
Async XLA Ops:
  0.6 1.3 %copy-start = (f32[256,9,128]{2,0,1:T(8,128)S(1)}, f32[256,9,128]{2,0,1:T(8,128)}, u32[]{:S(2)}) copy-start(f32[256,9,128]{2,0,1:T(8,128)} %param.6) | copy-start | bytes 3538948
  1.9 0.9 %copy-start.1 = (bf16[320,384]{1,0:T(8,128)(2,1)S(1)}, bf16[320,384]{1,0:T(8,128)(2,1)}, u32[]{:S(2)}) copy-start(bf16[320,384]{1,0:T(8,128)(2,1)} %constant.5.clone.perm_hbm) | copy-start | bytes 737284
  2.8 0.8 %copy-start.2 = (bf16[256,128]{1,0:T(8,128)(2,1)S(1)}, bf16[256,128]{1,0:T(8,128)(2,1)}, u32[]{:S(2)}) copy-start(bf16[256,128]{1,0:T(8,128)(2,1)} %constant.4.clone.spread_hbm) | copy-start | bytes 196612
  3.7 0.7 %copy-start.3 = (s32[256]{0:T(256)S(1)}, s32[256]{0:T(256)}, u32[]{:S(2)}) copy-start(s32[256]{0:T(256)} %param.9) | copy-start | bytes 3076
  4.4 0.7 %copy-start.4 = (s32[1,32]{1,0:T(1,128)S(1)}, s32[1,32]{1,0:T(1,128)}, u32[]{:S(2)}) copy-start(s32[1,32]{1,0:T(1,128)} %count_hbm.1) | copy-start | bytes 388
  5.0 0.7 %copy-start.5 = (s32[1,32]{1,0:T(1,128)S(1)}, s32[1,32]{1,0:T(1,128)}, u32[]{:S(2)}) copy-start(s32[1,32]{1,0:T(1,128)} %offset_hbm.1) | copy-start | bytes 388

commit v3 on v2

--- a/solution.py
+++ b/solution.py
@@ -279,7 +279,7 @@
     lax.fori_loop(0, blocks // 16, to_root, 0)
     (tiles,) = gather_same([acc[...] * 2.0 ** (-levels / 2)], same, spread_ref[...], lane8)
     own = jnp.concatenate(
-        [jnp.sum(t, axis=0, keepdims=True) for t in tiles] + [jnp.zeros((5, 128), F32)], axis=0
+        [jnp.sum(t, axis=0, keepdims=True) for t in tiles] + [jnp.zeros((1, 128), F32)], axis=0
     )
     root_send[...] = own
 
@@ -355,8 +355,8 @@
             pltpu.VMEM((8 * MONOS, 128), F32),
             pltpu.VMEM((devices, ROWS, 128), F32),
             pltpu.VMEM((devices, ROWS, 128), F32),
-            pltpu.VMEM((8, 128), F32),
-            pltpu.VMEM((devices, 8, 128), F32),
+            pltpu.VMEM((4, 128), F32),
+            pltpu.VMEM((devices, 4, 128), F32),
             dma((6,)),
             dma((devices,)),
             dma((devices,)),
@@ -364,7 +364,7 @@
             dma((devices,)),
         ],
         compiler_params=pltpu.CompilerParams(
-            collective_id=0, has_side_effects=True, vmem_limit_bytes=40 * 1024 * 1024
+            collective_id=0, has_side_effects=True, vmem_limit_bytes=63 * 1024 * 1024
         ),
         cost_estimate=pl.CostEstimate(
             flops=2 * blocks * 128 * COEFFS * 2, bytes_accessed=blocks * 128 * 40, transcendentals=0

time: 35.7 us -> 31.5 us (0.88)
  local copies, waits for them, and re-layouts: 6.26 us -> 2.82 us
  Pallas kernels: 28.5 us -> 27.9 us
    unnamed x14 -> x2, local copies, waits for them, and re-layouts: 6.26 us -> 2.82 us
    pallas_call x1, Pallas kernels: 28.5 us -> 27.9 us  [local(): pl.pallas_call(functools.partial(kernel, devices, low_size, cap), out_sha...]
where the time goes in v3:
time: 31.5 us; the launch traced here: 31.3 us
  Pallas kernels  27.9 us (89%)
  local copies, waits for them, and re-layouts  2.82 us (9%)
  between operations  0.64 us (2%)
    pallas_call x1, Pallas kernels, local(): pl.pallas_call(functools.partial(kernel, devices, low_size, cap), out_sha...  27.9 us
    unnamed x2, local copies, waits for them, and re-layouts  2.82 us

profile of v3, /device:TPU:0, one launch (start us, length us, event | category | flops | bytes accessed | tf_op | source)
XLA Modules:
  0.0 31.3 jit_solution(11560869077347592226)
XLA Ops:
  0.6 27.9 %shard_map.77 = (f32[315,128]{1,0:T(8,128)}, f32[1,315]{1,0:T(1,128)}) custom-call(f32[9,256,128]{2,1,0:T(8,128)} %bitcast.2, s32[2,128]{1,0:T(2,128)} %bitcast.3, bf16[320,384]{1,0:T(8,128)(2,1)} %constant.5.clone.perm_hbm, bf16[256,128]{1,0:T(8,128)(2,1)} %constant.4.clone.spread_hbm, s32[1,32]{1,0:T(1,128)} %count_hbm.1, s32[1,32]{1,0:T(1,128)} %offset_hbm.1), custom_call_target="tpu_custom_call" | custom-call | flops 41287680 | bytes 1310720 | tf_op jit(solution)/shard_map/pallas_call | solution.py:338
  28.5 1.6 %copy.10 = f32[315,128]{1,0:T(8,128)} copy(f32[315,128]{1,0:T(8,128)} %get-tuple-element.4) | data formatting | bytes 322560
  30.1 1.2 %copy.11 = f32[1,315]{1,0:T(1,128)} copy(f32[1,315]{1,0:T(1,128)} %get-tuple-element.5) | data formatting | bytes 2520

commit v4 on v3

--- a/solution.py
+++ b/solution.py
@@ -114,26 +114,25 @@
     leaf_out, root_out,
     seg_ref, leaf_ref, perm_ref, spread_ref, count_ref, offset_ref,
     place, moments, acc, sbuf, rbuf, root_send, root_recv,
-    load_sem, send_sem, recv_sem, root_send_sem, root_recv_sem,
+    leaf_made, root_made,
+    load_sem, send_sem, recv_sem, root_send_sem, root_recv_sem, out_sem,
 ):
+    blocks = seg_ref.shape[1]
+    eighth = blocks // 8
+    pieces = [pl.ds(0, 2 * eighth), pl.ds(6 * eighth, 2 * eighth), pl.ds(2 * eighth, 4 * eighth)]
     fetches = [
         pltpu.make_async_copy(src, dst, load_sem.at[i])
         for i, (src, dst) in enumerate(
-            (
-                (leaf_hbm, leaf_ref),
-                (seg_hbm, seg_ref),
-                (spread_hbm, spread_ref),
-                (count_hbm, count_ref),
-                (offset_hbm, offset_ref),
-                (perm_hbm, perm_ref),
-            )
+            [(leaf_hbm, leaf_ref)]
+            + [(seg_hbm.at[:, p], seg_ref.at[:, p]) for p in pieces[:2]]
+            + [(spread_hbm, spread_ref), (count_hbm, count_ref), (offset_hbm, offset_ref)]
+            + [(seg_hbm.at[:, pieces[2]], seg_ref.at[:, pieces[2]]), (perm_hbm, perm_ref)]
         )
     ]
     for fetch in fetches:
         fetch.start()
 
     me = lax.axis_index("top") * low_size + lax.axis_index("low")
-    blocks = seg_ref.shape[1]
 
     def partner(step):
         other = lax.rem(me + step, devices)
@@ -155,7 +154,7 @@
         place[3, chunk * 128 : chunk * 128 + 128] = column(
             leaves[chunk : chunk + 1].astype(F32)
         )
-    for fetch in fetches[1:5]:
+    for fetch in fetches[1:6]:
         fetch.wait()
 
     lane8 = lax.broadcasted_iota(jnp.int32, (8, 128), 1)
@@ -213,32 +212,38 @@
             device_id=partner(step)[1], device_id_type=MESH,
         )
 
-    quarter = blocks // 4
-    ready = quarter // cap
-    turns = quarter // (8 * TOGETHER)
+    ready = eighth // cap
+    turns = eighth // (8 * TOGETHER)
+
+    def send_early(done):
+        def body(turn, carry):
+            spot = lax.rem(me + turn, 2 * ready)
+            owner = jnp.where(spot < ready, spot + done, devices - 2 * ready + spot - done)
+            step = lax.rem(owner - me + devices, devices)
+
+            @pl.when(step != 0)
+            def _():
+                put(sbuf, step, packed(owner))
+                block_copy(step).start()
+
+            return carry
+
+        return body
+
     lax.fori_loop(0, turns, p2m(0), 0)
-    lax.fori_loop(0, turns, p2m(3 * quarter // 8), 0)
+    lax.fori_loop(0, turns, p2m(7 * eighth // 8), 0)
     pl.semaphore_wait(barrier, devices - 1)
-
-    def send_early(turn, carry):
-        spot = lax.rem(me + turn, 2 * ready)
-        owner = jnp.where(spot < ready, spot, devices - 2 * ready + spot)
-        step = lax.rem(owner - me + devices, devices)
-
-        @pl.when(step != 0)
-        def _():
-            put(sbuf, step, packed(owner))
-            block_copy(step).start()
-
-        return carry
-
-    lax.fori_loop(0, 2 * ready, send_early, 0)
-    lax.fori_loop(0, 2 * turns, p2m(quarter // 8), 0)
+    lax.fori_loop(0, 2 * ready, send_early(0), 0)
+    lax.fori_loop(0, turns, p2m(eighth // 8), 0)
+    lax.fori_loop(0, turns, p2m(6 * eighth // 8), 0)
+    lax.fori_loop(0, 2 * ready, send_early(ready), 0)
+    fetches[6].wait()
+    lax.fori_loop(0, 4 * turns, p2m(2 * eighth // 8), 0)
 
     def send_late(step, carry):
         owner = partner(step)[0]
 
-        @pl.when((owner >= ready) & (owner < devices - ready))
+        @pl.when((owner >= 2 * ready) & (owner < devices - 2 * ready))
         def _():
             put(sbuf, step, packed(owner))
             block_copy(step).start()
@@ -293,25 +298,26 @@
         block_copy(step).wait()
         return carry
 
-    part = devices // 2
-    half_rows = part * 8
-    flat = lambda x: x.reshape(half_rows, 128)
-    leaf_lane = lax.broadcasted_iota(jnp.int32, (half_rows, 128), 1).astype(F32)
     cells = jnp.zeros((LEAF_DEV, 384), F32)
-    for start in (0, part):
-        lax.fori_loop(max(start, 1), start + part, take, 0)
-        got = pl.ds(start, part)
-        near = [flat(rbuf[got, 0:8]), flat(rbuf[got, 16:24]), flat(rbuf[got, 32:40])]
-        far = [flat(rbuf[got, 8:16]), flat(rbuf[got, 24:32]), pltpu.roll(near[2], 64, 1)]
-        for side in (near, far):
+    bounds = [0, devices // 2, devices // 8 * 7, devices]
+    for start, end in zip(bounds[:-1], bounds[1:]):
+        lax.fori_loop(max(start, 1), end, take, 0)
+        rows = (end - start) * 8
+        leaf_lane = lax.broadcasted_iota(jnp.int32, (rows, 128), 1).astype(F32)
+        got = [
+            rbuf[start:end, at : at + 8].reshape(rows, 128) for at in range(0, ROWS, 8)
+        ]
+        for side in (got[0::2], [got[1], got[3], pltpu.roll(got[4], 64, 1)]):
             hit = jnp.where(side[2][:, 63:64] == leaf_lane, 1.0, 0.0)
             hit = jnp.transpose(hit).astype(BF16)
             high, low = split(jnp.concatenate(side, axis=1))
             cells = cells + dot(hit, high, NN) + dot(hit, low, NN)
-    fetches[5].wait()
+    fetches[7].wait()
     perm = perm_ref[...]
     high, low = split(cells)
-    leaf_out[...] = (dot(perm, high, NT) + dot(perm, low, NT))[:COEFFS]
+    leaf_made[...] = (dot(perm, high, NT) + dot(perm, low, NT))[:COEFFS]
+    leaf_store = pltpu.make_async_copy(leaf_made, leaf_out, out_sem.at[0])
+    leaf_store.start()
 
     def take_root(step, carry):
         root_copy(step).wait()
@@ -322,7 +328,24 @@
     total = jnp.sum(root_recv[...], axis=0)
     line = jnp.concatenate([total[0:1], total[1:2], total[2:3]], axis=1)
     high, low = split(jnp.broadcast_to(line, (16, 384)))
-    root_out[...] = (dot(high, perm, NT) + dot(low, perm, NT))[0:1, :COEFFS]
+    root_made[...] = (dot(high, perm, NT) + dot(low, perm, NT))[0:1, :COEFFS]
+    root_store = pltpu.make_async_copy(root_made, root_out, out_sem.at[1])
+    root_store.start()
+    leaf_store.wait()
+    root_store.wait()
+
+
+def hand_over(leaf_in, root_in, leaf_out, root_out, sem):
+    cuts = [0, 80, 160, 240, COEFFS]
+    copies = [
+        pltpu.make_async_copy(leaf_in.at[a:b], leaf_out.at[a:b], sem.at[i])
+        for i, (a, b) in enumerate(zip(cuts[:-1], cuts[1:]))
+    ]
+    copies.append(pltpu.make_async_copy(root_in, root_out, sem.at[4]))
+    for copy in copies:
+        copy.start()
+    for copy in copies:
+        copy.wait()
 
 
 def local(devices, low_size, segments, send_counts, send_offsets, leaf_of_block):
@@ -331,18 +354,18 @@
     one = ((lanes[None, :] % 9 == lanes[:, None] // 8) & (lanes[:, None] < 72)).astype(np.float32)
     spread = jnp.asarray(np.concatenate([one, one], axis=0), BF16)
     perm = jnp.asarray(make_permutation(), BF16)
-    vmem = pl.BlockSpec(memory_space=pltpu.VMEM)
     hbm = pl.BlockSpec(memory_space=pltpu.HBM)
     cap = max(2, 2 * blocks // devices)
     dma = pltpu.SemaphoreType.DMA
-    return pl.pallas_call(
+    shapes = (
+        jax.ShapeDtypeStruct((COEFFS, LEAF_DEV), F32),
+        jax.ShapeDtypeStruct((1, COEFFS), F32),
+    )
+    results = pl.pallas_call(
         functools.partial(kernel, devices, low_size, cap),
-        out_shape=(
-            jax.ShapeDtypeStruct((COEFFS, LEAF_DEV), F32),
-            jax.ShapeDtypeStruct((1, COEFFS), F32),
-        ),
+        out_shape=shapes,
         in_specs=[hbm] * 6,
-        out_specs=(vmem, vmem),
+        out_specs=(hbm, hbm),
         scratch_shapes=[
             pltpu.VMEM((9, blocks, 128), F32),
             pltpu.VMEM((blocks // 128, 128), jnp.int32),
@@ -357,11 +380,14 @@
             pltpu.VMEM((devices, ROWS, 128), F32),
             pltpu.VMEM((4, 128), F32),
             pltpu.VMEM((devices, 4, 128), F32),
-            dma((6,)),
+            pltpu.VMEM((COEFFS, LEAF_DEV), F32),
+            pltpu.VMEM((1, COEFFS), F32),
+            dma((8,)),
             dma((devices,)),
             dma((devices,)),
             dma((devices,)),
             dma((devices,)),
+            dma((2,)),
         ],
         compiler_params=pltpu.CompilerParams(
             collective_id=0, has_side_effects=True, vmem_limit_bytes=63 * 1024 * 1024
@@ -377,6 +403,14 @@
         send_counts,
         send_offsets,
     )
+    return pl.pallas_call(
+        hand_over,
+        out_shape=shapes,
+        in_specs=[hbm, hbm],
+        out_specs=(hbm, hbm),
+        scratch_shapes=[dma((5,))],
+        compiler_params=pltpu.CompilerParams(vmem_limit_bytes=63 * 1024 * 1024),
+    )(*results)
 
 
 def solution(mesh):

time: 31.5 us -> 34 us (1.079)
  Pallas kernels: 27.9 us -> 33.2 us
  local copies, waits for them, and re-layouts: 2.82 us -> 0 us
    pallas_call x0 -> x1, Pallas kernels: none -> 6.08 us  [local(): pl.pallas_call(hand_over, out_shape=shapes, in_specs=[hbm, hbm], out_spec...]
    unnamed x2 -> x0, local copies, waits for them, and re-layouts: 2.82 us -> none
    pallas_call x1, Pallas kernels: 27.9 us -> 27.1 us  [local(): pl.pallas_call(functools.partial(kernel, devices, low_size, cap), out_sha...]
where the time goes in v4:
time: 34 us; the launch traced here: 33.8 us
  Pallas kernels  33.2 us (98%)
  between operations  0.64 us (2%)
    pallas_call x1, Pallas kernels, local(): pl.pallas_call(functools.partial(kernel, devices, low_size, cap), out_sha...  27.1 us
    pallas_call x1, Pallas kernels, local(): pl.pallas_call(hand_over, out_shape=shapes, in_specs=[hbm, hbm], out_spec...  6.08 us

profile of v4, /device:TPU:0, one launch (start us, length us, event | category | flops | bytes accessed | tf_op | source)
XLA Modules:
  0.0 33.8 jit_solution(14557082362904487483)
XLA Ops:
  0.6 27.1 %shard_map.77 = (f32[315,128]{1,0:T(8,128)}, f32[1,315]{1,0:T(1,128)}) custom-call(f32[9,256,128]{2,1,0:T(8,128)} %bitcast.2, s32[2,128]{1,0:T(2,128)} %bitcast.3, bf16[320,384]{1,0:T(8,128)(2,1)} %constant.5.clone.perm_hbm, bf16[256,128]{1,0:T(8,128)(2,1)} %constant.4.clone.spread_hbm, s32[1,32]{1,0:T(1,128)} %count_hbm.1, s32[1,32]{1,0:T(1,128)} %offset_hbm.1), custom_call_target="tpu_custom_call" | custom-call | flops 41287680 | bytes 1310720 | tf_op jit(solution)/shard_map/pallas_call | solution.py:364
  27.8 6.1 %shard_map.78 = (f32[315,128]{1,0:T(8,128)}, f32[1,315]{1,0:T(1,128)}) custom-call(f32[315,128]{1,0:T(8,128)} %get-tuple-element.4.leaf_in, f32[1,315]{1,0:T(1,128)} %get-tuple-element.5.root_in), custom_call_target="tpu_custom_call" | custom-call | tf_op jit(solution)/shard_map/pallas_call | solution.py:406

commit v5 on v4

--- a/solution.py
+++ b/solution.py
@@ -14,7 +14,6 @@
 LEAF_DEV = 128
 SLOTS = 16
 ROWS = 2 * SLOTS + SLOTS // 2
-TOGETHER = 4
 MESH = pl.DeviceIdType.MESH
 BF16 = jnp.bfloat16
 F32 = jnp.float32
@@ -109,24 +108,27 @@
 
 
 def kernel(
-    devices, low_size, cap,
+    devices, low_size,
     seg_hbm, leaf_hbm, perm_hbm, spread_hbm, count_hbm, offset_hbm,
     leaf_out, root_out,
     seg_ref, leaf_ref, perm_ref, spread_ref, count_ref, offset_ref,
-    place, moments, acc, sbuf, rbuf, root_send, root_recv,
+    place, acc, sbuf, rbuf, root_send, root_recv,
     leaf_made, root_made,
     load_sem, send_sem, recv_sem, root_send_sem, root_recv_sem, out_sem,
 ):
-    blocks = seg_ref.shape[1]
-    eighth = blocks // 8
-    pieces = [pl.ds(0, 2 * eighth), pl.ds(6 * eighth, 2 * eighth), pl.ds(2 * eighth, 4 * eighth)]
+    blocks = seg_ref.shape[1] - SLOTS
+    body_rows = pl.ds(0, blocks)
     fetches = [
         pltpu.make_async_copy(src, dst, load_sem.at[i])
         for i, (src, dst) in enumerate(
-            [(leaf_hbm, leaf_ref)]
-            + [(seg_hbm.at[:, p], seg_ref.at[:, p]) for p in pieces[:2]]
-            + [(spread_hbm, spread_ref), (count_hbm, count_ref), (offset_hbm, offset_ref)]
-            + [(seg_hbm.at[:, pieces[2]], seg_ref.at[:, pieces[2]]), (perm_hbm, perm_ref)]
+            (
+                (leaf_hbm, leaf_ref),
+                (seg_hbm, seg_ref.at[:, body_rows]),
+                (spread_hbm, spread_ref),
+                (count_hbm, count_ref),
+                (offset_hbm, offset_ref),
+                (perm_hbm, perm_ref),
+            )
         )
     ]
     for fetch in fetches:
@@ -145,7 +147,8 @@
         return carry
 
     lax.fori_loop(1, devices, greet, 0)
-    moments[...] = jnp.zeros_like(moments)
+    seg_ref[:, blocks:] = jnp.zeros((9, SLOTS, 128), F32)
+    place[:, blocks:] = jnp.zeros((4, SLOTS, 128), F32)
     acc[...] = jnp.zeros_like(acc)
 
     fetches[0].wait()
@@ -154,49 +157,18 @@
         place[3, chunk * 128 : chunk * 128 + 128] = column(
             leaves[chunk : chunk + 1].astype(F32)
         )
-    for fetch in fetches[1:6]:
+    for fetch in fetches[1:5]:
         fetch.wait()
 
     lane8 = lax.broadcasted_iota(jnp.int32, (8, 128), 1)
     row8 = lax.broadcasted_iota(jnp.int32, (8, 128), 0)
     same = jnp.where(lax.rem(lane8, 8) == row8, 1.0, 0.0)
 
-    def load(group):
-        rows = pl.ds(pl.multiple_of(group * 8, 8), 8)
+    def load(rows):
         parts = [seg_ref[c, rows, :] for c in range(9)]
         scaled = [h * (2.0 / math.sqrt(128.0)) for h in parts[6:9]]
         tensors = [b * h for b in parts[0:3] for h in scaled]
-        return rows, parts[3:6], parts[6:9], tensors
-
-    def p2m(first_group):
-        def body(turn, carry):
-            products, places = [], []
-            for u in range(TOGETHER):
-                rows, middle, half, tensors = load(first_group + turn * TOGETHER + u)
-                products.append(pair_products(monomials(middle, half), tensors))
-                places.append(rows)
-            for rows, tiles in zip(places, gather_same(products, same, spread_ref[...], lane8)):
-                moments[0, rows, :] = tiles[0]
-                moments[1, rows, :] = tiles[1]
-                moments[2, rows, :] = jnp.where(lane8 == 63, place[3, rows, :], tiles[2])
-            return carry
-
-        return body
-
-    lane16 = lax.broadcasted_iota(jnp.int32, (SLOTS, 128), 1)
-    slot16 = lax.broadcasted_iota(jnp.int32, (SLOTS, 128), 0)
-
-    def packed(owner):
-        rows = pl.ds(offset_ref[0, owner], SLOTS)
-        dead = (lane16 == 63) & (slot16 >= count_ref[0, owner])
-        third = jnp.where(dead, -1.0, moments[2, rows, :])
-        folded = jnp.where(lane8 < 64, third[:8], pltpu.roll(third[8:], 64, 1))
-        return moments[0, rows, :], moments[1, rows, :], folded
-
-    def put(ref, step, pieces):
-        ref[step, 0:SLOTS, :] = pieces[0]
-        ref[step, SLOTS : 2 * SLOTS, :] = pieces[1]
-        ref[step, 2 * SLOTS : ROWS, :] = pieces[2]
+        return parts[3:6], parts[6:9], tensors
 
     def block_copy(step):
         return pltpu.make_async_remote_copy(
@@ -212,46 +184,39 @@
             device_id=partner(step)[1], device_id_type=MESH,
         )
 
-    ready = eighth // cap
-    turns = eighth // (8 * TOGETHER)
-
-    def send_early(done):
-        def body(turn, carry):
-            spot = lax.rem(me + turn, 2 * ready)
-            owner = jnp.where(spot < ready, spot + done, devices - 2 * ready + spot - done)
-            step = lax.rem(owner - me + devices, devices)
+    pl.semaphore_wait(barrier, devices - 1)
+
+    def send(turn, carry):
+        steps, products, leaf_rows = [], [], []
+        for u in range(2):
+            step = lax.rem(turn * 2 + u + 1, devices)
+            owner = partner(step)[0]
+            for side in (0, 8):
+                rows = pl.ds(offset_ref[0, owner] + side, 8)
+                middle, half, tensors = load(rows)
+                products.append(pair_products(monomials(middle, half), tensors))
+                leaf = jnp.where(row8 + side < count_ref[0, owner], place[3, rows, :], -1.0)
+                leaf_rows.append(leaf)
+            steps.append(step)
+        made = gather_same(products, same, spread_ref[...], lane8)
+        for u, step in enumerate(steps):
+            near, far = made[2 * u : 2 * u + 2]
+            last_near = jnp.where(lane8 == 63, leaf_rows[2 * u], near[2])
+            last_far = jnp.where(lane8 == 63, leaf_rows[2 * u + 1], far[2])
+            sbuf[step, 0:8, :] = near[0]
+            sbuf[step, 8:16, :] = far[0]
+            sbuf[step, 16:24, :] = near[1]
+            sbuf[step, 24:32, :] = far[1]
+            sbuf[step, 32:40, :] = jnp.where(lane8 < 64, last_near, pltpu.roll(last_far, 64, 1))
 
             @pl.when(step != 0)
             def _():
-                put(sbuf, step, packed(owner))
                 block_copy(step).start()
 
-            return carry
-
-        return body
-
-    lax.fori_loop(0, turns, p2m(0), 0)
-    lax.fori_loop(0, turns, p2m(7 * eighth // 8), 0)
-    pl.semaphore_wait(barrier, devices - 1)
-    lax.fori_loop(0, 2 * ready, send_early(0), 0)
-    lax.fori_loop(0, turns, p2m(eighth // 8), 0)
-    lax.fori_loop(0, turns, p2m(6 * eighth // 8), 0)
-    lax.fori_loop(0, 2 * ready, send_early(ready), 0)
-    fetches[6].wait()
-    lax.fori_loop(0, 4 * turns, p2m(2 * eighth // 8), 0)
-
-    def send_late(step, carry):
-        owner = partner(step)[0]
-
-        @pl.when((owner >= 2 * ready) & (owner < devices - 2 * ready))
-        def _():
-            put(sbuf, step, packed(owner))
-            block_copy(step).start()
-
-        return carry
-
-    lax.fori_loop(1, devices, send_late, 0)
-    put(rbuf, 0, packed(me))
+        return carry
+
+    lax.fori_loop(0, devices // 2, send, 0)
+    rbuf[0] = sbuf[0]
 
     levels = LEAF_DEV.bit_length() - 1 + devices.bit_length() - 1
     depth = [len(range(d, levels, 3)) for d in range(3)]
@@ -273,7 +238,8 @@
         shrink = [0.5**k for k in depth]
         total = None
         for u in range(2):
-            rows, middle, half, tensors = load(turn * 2 + u)
+            rows = pl.ds(pl.multiple_of(turn * 16 + u * 8, 8), 8)
+            middle, half, tensors = load(rows)
             middle = [(p + place[d, rows, :]) * shrink[d] for d, p in enumerate(middle)]
             half = [h * shrink[d] for d, h in enumerate(half)]
             products = pair_products(monomials(middle, half), tensors)
@@ -312,7 +278,7 @@
             hit = jnp.transpose(hit).astype(BF16)
             high, low = split(jnp.concatenate(side, axis=1))
             cells = cells + dot(hit, high, NN) + dot(hit, low, NN)
-    fetches[7].wait()
+    fetches[5].wait()
     perm = perm_ref[...]
     high, low = split(cells)
     leaf_made[...] = (dot(perm, high, NT) + dot(perm, low, NT))[:COEFFS]
@@ -335,16 +301,21 @@
     root_store.wait()
 
 
-def hand_over(leaf_in, root_in, leaf_out, root_out, sem):
-    cuts = [0, 80, 160, 240, COEFFS]
-    copies = [
-        pltpu.make_async_copy(leaf_in.at[a:b], leaf_out.at[a:b], sem.at[i])
-        for i, (a, b) in enumerate(zip(cuts[:-1], cuts[1:]))
+def hand_over(leaf_in, root_in, leaf_out, root_out, leaf_held, root_held, sem):
+    incoming = [
+        pltpu.make_async_copy(leaf_in, leaf_held, sem.at[0]),
+        pltpu.make_async_copy(root_in, root_held, sem.at[1]),
     ]
-    copies.append(pltpu.make_async_copy(root_in, root_out, sem.at[4]))
-    for copy in copies:
+    outgoing = [
+        pltpu.make_async_copy(leaf_held, leaf_out, sem.at[2]),
+        pltpu.make_async_copy(root_held, root_out, sem.at[3]),
+    ]
+    for copy in incoming:
         copy.start()
-    for copy in copies:
+    for first, then in zip(incoming, outgoing):
+        first.wait()
+        then.start()
+    for copy in outgoing:
         copy.wait()
 
 
@@ -355,26 +326,24 @@
     spread = jnp.asarray(np.concatenate([one, one], axis=0), BF16)
     perm = jnp.asarray(make_permutation(), BF16)
     hbm = pl.BlockSpec(memory_space=pltpu.HBM)
-    cap = max(2, 2 * blocks // devices)
     dma = pltpu.SemaphoreType.DMA
     shapes = (
         jax.ShapeDtypeStruct((COEFFS, LEAF_DEV), F32),
         jax.ShapeDtypeStruct((1, COEFFS), F32),
     )
     results = pl.pallas_call(
-        functools.partial(kernel, devices, low_size, cap),
+        functools.partial(kernel, devices, low_size),
         out_shape=shapes,
         in_specs=[hbm] * 6,
         out_specs=(hbm, hbm),
         scratch_shapes=[
-            pltpu.VMEM((9, blocks, 128), F32),
+            pltpu.VMEM((9, blocks + SLOTS, 128), F32),
             pltpu.VMEM((blocks // 128, 128), jnp.int32),
             pltpu.VMEM((320, 384), BF16),
             pltpu.VMEM((256, 128), BF16),
             pltpu.SMEM((1, devices), jnp.int32),
             pltpu.SMEM((1, devices), jnp.int32),
-            pltpu.VMEM((4, blocks, 128), F32),
-            pltpu.VMEM((3, blocks + SLOTS, 128), F32),
+            pltpu.VMEM((4, blocks + SLOTS, 128), F32),
             pltpu.VMEM((8 * MONOS, 128), F32),
             pltpu.VMEM((devices, ROWS, 128), F32),
             pltpu.VMEM((devices, ROWS, 128), F32),
@@ -382,7 +351,7 @@
             pltpu.VMEM((devices, 4, 128), F32),
             pltpu.VMEM((COEFFS, LEAF_DEV), F32),
             pltpu.VMEM((1, COEFFS), F32),
-            dma((8,)),
+            dma((6,)),
             dma((devices,)),
             dma((devices,)),
             dma((devices,)),
@@ -408,7 +377,11 @@
         out_shape=shapes,
         in_specs=[hbm, hbm],
         out_specs=(hbm, hbm),
-        scratch_shapes=[dma((5,))],
+        scratch_shapes=[
+            pltpu.VMEM((COEFFS, LEAF_DEV), F32),
+            pltpu.VMEM((1, COEFFS), F32),
+            dma((4,)),
+        ],
         compiler_params=pltpu.CompilerParams(vmem_limit_bytes=63 * 1024 * 1024),
     )(*results)
 

time: 34 us -> 30.3 us (0.89)
  Pallas kernels: 33.2 us -> 29.5 us
    pallas_call x1, Pallas kernels: 6.08 us -> 1.62 us  [local(): pl.pallas_call(hand_over, out_shape=shapes, in_specs=[hbm, hbm], out_spec...]
    pallas_call x1, Pallas kernels: 27.1 us -> 27.8 us  [local(): pl.pallas_call(functools.partial(kernel, devices, low_size), out_shape=sh...]
where the time goes in v5:
time: 30.3 us; the launch traced here: 30.1 us
  Pallas kernels  29.5 us (97%)
  between operations  0.64 us (2%)
    pallas_call x1, Pallas kernels, local(): pl.pallas_call(functools.partial(kernel, devices, low_size), out_shape=sh...  27.8 us
    pallas_call x1, Pallas kernels, local(): pl.pallas_call(hand_over, out_shape=shapes, in_specs=[hbm, hbm], out_spec...  1.62 us

profile of v5, /device:TPU:0, one launch (start us, length us, event | category | flops | bytes accessed | tf_op | source)
XLA Modules:
  0.0 30.1 jit_solution(15224732143885391382)
XLA Ops:
  0.6 27.8 %shard_map.77 = (f32[315,128]{1,0:T(8,128)}, f32[1,315]{1,0:T(1,128)}) custom-call(f32[9,256,128]{2,1,0:T(8,128)} %bitcast.2, s32[2,128]{1,0:T(2,128)} %bitcast.3, bf16[320,384]{1,0:T(8,128)(2,1)} %constant.5.clone.perm_hbm, bf16[256,128]{1,0:T(8,128)(2,1)} %constant.4.clone.spread_hbm, s32[1,32]{1,0:T(1,128)} %count_hbm.1, s32[1,32]{1,0:T(1,128)} %offset_hbm.1), custom_call_target="tpu_custom_call" | custom-call | flops 41287680 | bytes 1310720 | tf_op jit(solution)/shard_map/pallas_call | solution.py:334
  28.5 1.6 %shard_map.78 = (f32[315,128]{1,0:T(8,128)}, f32[1,315]{1,0:T(1,128)}) custom-call(f32[315,128]{1,0:T(8,128)} %get-tuple-element.4.leaf_in, f32[1,315]{1,0:T(1,128)} %get-tuple-element.5.root_in), custom_call_target="tpu_custom_call" | custom-call | tf_op jit(solution)/shard_map/pallas_call | solution.py:375

commit v6 on v5

--- a/solution.py
+++ b/solution.py
@@ -46,6 +46,30 @@
         for a in range(9):
             table[MONOS * a + m, 128 * (m // 14) + 9 * (m % 14) + a] = 1.0
     return table
+
+
+def make_shift_tiles(depth, scale):
+    tiles, places = [], []
+    for target in EXPONENTS:
+        table = np.zeros((40, 384), np.float32)
+        for n, source in enumerate(EXPONENTS):
+            rest = tuple(t - s for t, s in zip(target, source))
+            if min(rest) < 0:
+                continue
+            factor = scale
+            for t, s, d in zip(target, source, depth):
+                factor *= math.comb(t, s) * 2.0 ** (-d * s)
+            lane = 128 * (n // 14) + 9 * (n % 14)
+            table[EXPONENTS.index(rest), lane : lane + 9] = factor
+        found = []
+        for i in range(5):
+            for j in range(3):
+                tile = table[8 * i : 8 * i + 8, 128 * j : 128 * j + 128]
+                if tile.any():
+                    found.append((i, j, len(tiles)))
+                    tiles.append(tile)
+        places.append(found)
+    return np.stack(tiles), places
 
 
 def split(x):
@@ -76,10 +100,10 @@
 
 def pair_products(quads, tensors):
     q_high, q_low = split(jnp.concatenate(quads, axis=0))
-    t_high, t_low = split(jnp.concatenate(tensors + [jnp.zeros((56, 128), F32)], axis=0))
+    stacked = jnp.concatenate(tensors + [jnp.zeros((56, 128), F32)], axis=0)
+    right = jnp.concatenate(split(jnp.transpose(stacked)), axis=1)
     left = jnp.concatenate([q_high, q_low], axis=1)
-    right = jnp.concatenate([t_high, t_low], axis=0)
-    both = dot(left, jnp.concatenate([right, right], axis=1), NT)
+    both = dot(left, jnp.concatenate([right, right], axis=0), NN)
     return both[:, :128] + both[:, 128:]
 
 
@@ -108,11 +132,11 @@
 
 
 def kernel(
-    devices, low_size,
-    seg_hbm, leaf_hbm, perm_hbm, spread_hbm, count_hbm, offset_hbm,
+    devices, low_size, depth, tile_places,
+    seg_hbm, leaf_hbm, perm_hbm, spread_hbm, count_hbm, offset_hbm, shift_hbm, power_hbm,
     leaf_out, root_out,
-    seg_ref, leaf_ref, perm_ref, spread_ref, count_ref, offset_ref,
-    place, acc, sbuf, rbuf, root_send, root_recv,
+    seg_ref, leaf_ref, perm_ref, spread_ref, count_ref, offset_ref, shift_ref, power_ref,
+    place, sbuf, rbuf, root_send, root_recv,
     leaf_made, root_made,
     load_sem, send_sem, recv_sem, root_send_sem, root_recv_sem, out_sem,
 ):
@@ -128,6 +152,8 @@
                 (count_hbm, count_ref),
                 (offset_hbm, offset_ref),
                 (perm_hbm, perm_ref),
+                (shift_hbm, shift_ref),
+                (power_hbm, power_ref),
             )
         )
     ]
@@ -148,13 +174,12 @@
 
     lax.fori_loop(1, devices, greet, 0)
     seg_ref[:, blocks:] = jnp.zeros((9, SLOTS, 128), F32)
-    place[:, blocks:] = jnp.zeros((4, SLOTS, 128), F32)
-    acc[...] = jnp.zeros_like(acc)
+    place[blocks:] = jnp.zeros((SLOTS, 128), F32)
 
     fetches[0].wait()
     leaves = leaf_ref[...]
     for chunk in range(blocks // 128):
-        place[3, chunk * 128 : chunk * 128 + 128] = column(
+        place[chunk * 128 : chunk * 128 + 128] = column(
             leaves[chunk : chunk + 1].astype(F32)
         )
     for fetch in fetches[1:5]:
@@ -195,10 +220,10 @@
                 rows = pl.ds(offset_ref[0, owner] + side, 8)
                 middle, half, tensors = load(rows)
                 products.append(pair_products(monomials(middle, half), tensors))
-                leaf = jnp.where(row8 + side < count_ref[0, owner], place[3, rows, :], -1.0)
+                leaf = jnp.where(row8 + side < count_ref[0, owner], place[rows, :], -1.0)
                 leaf_rows.append(leaf)
             steps.append(step)
-        made = gather_same(products, same, spread_ref[...], lane8)
+        made = gather_same(products, same, spread_ref[0], lane8)
         for u, step in enumerate(steps):
             near, far = made[2 * u : 2 * u + 2]
             last_near = jnp.where(lane8 == 63, leaf_rows[2 * u], near[2])
@@ -218,37 +243,44 @@
     lax.fori_loop(0, devices // 2, send, 0)
     rbuf[0] = sbuf[0]
 
-    levels = LEAF_DEV.bit_length() - 1 + devices.bit_length() - 1
-    depth = [len(range(d, levels, 3)) for d in range(3)]
-    for chunk in range(blocks // 128):
-        index = lax.broadcasted_iota(jnp.int32, (1, 128), 1) + chunk * 128
-        owner = jnp.zeros((1, 128), jnp.int32)
-        for o in range(devices):
-            end = offset_ref[0, o] + count_ref[0, o]
-            owner = owner + jnp.where(index >= end, 1, 0)
-        cell = owner * LEAF_DEV + leaves[chunk : chunk + 1]
+    def unfold(ref, start, end):
+        rows = (end - start) * 8
+        got = [ref[start:end, at : at + 8].reshape(rows, 128) for at in range(0, ROWS, 8)]
+        return got[0::2], [got[1], got[3], pltpu.roll(got[4], 64, 1)]
+
+    fetches[6].wait()
+    fetches[7].wait()
+    rows = devices * 8
+    shape = (rows, 128)
+    owner = me + lax.shift_right_logical(lax.broadcasted_iota(jnp.int32, shape, 0), 3)
+    owner = jnp.where(owner >= devices, owner - devices, owner)
+    powers = [power_ref[d : d + 1, :] for d in range(3)]
+    lane_used = lax.broadcasted_iota(jnp.int32, shape, 1) < MONOS
+    grown = jnp.zeros((128, 384), F32)
+    for side in unfold(sbuf, 0, devices):
+        leaf = jnp.broadcast_to(side[2][:, 63:64], shape)
+        cell = owner * LEAF_DEV + leaf.astype(jnp.int32)
+        factor = jnp.where((leaf >= 0.0) & lane_used, 1.0, 0.0)
         for d in range(3):
-            centre = jnp.zeros((1, 128), F32)
-            for level in range(d, levels, 3):
-                bit = lax.shift_right_logical(cell, level) & 1
-                centre = centre + jnp.where(bit == 1, 1.0, -1.0) * 2.0 ** (level // 3)
-            place[d, chunk * 128 : chunk * 128 + 128] = column(centre)
-
-    def to_root(turn, carry):
-        shrink = [0.5**k for k in depth]
+            bits = jnp.zeros(shape, jnp.int32)
+            for j in range(depth[d]):
+                moved = lax.shift_right_logical(cell, 2 * j + d) if 2 * j + d else cell
+                bits = bits | (moved & (1 << j))
+            centre = bits.astype(F32) * 2.0 ** (1 - depth[d]) - (1.0 - 2.0 ** -depth[d])
+            for least in range(1, 5):
+                factor = factor * jnp.where(powers[d] >= least, centre, 1.0)
+        c_high, c_low = split(jnp.transpose(factor))
+        high, low = split(jnp.concatenate(side, axis=1))
+        grown = grown + dot(c_high, high, NN) + dot(c_low, high, NN) + dot(c_high, low, NN)
+    sums = []
+    for found in tile_places:
         total = None
-        for u in range(2):
-            rows = pl.ds(pl.multiple_of(turn * 16 + u * 8, 8), 8)
-            middle, half, tensors = load(rows)
-            middle = [(p + place[d, rows, :]) * shrink[d] for d, p in enumerate(middle)]
-            half = [h * shrink[d] for d, h in enumerate(half)]
-            products = pair_products(monomials(middle, half), tensors)
-            total = products if total is None else total + products
-        acc[...] += total
-        return carry
-
-    lax.fori_loop(0, blocks // 16, to_root, 0)
-    (tiles,) = gather_same([acc[...] * 2.0 ** (-levels / 2)], same, spread_ref[...], lane8)
+        for i, j, at in found:
+            term = grown[8 * i : 8 * i + 8, 128 * j : 128 * j + 128] * shift_ref[at]
+            total = term if total is None else total + term
+        sums.append(total)
+    ones = jnp.ones((8, 128), F32)
+    (tiles,) = gather_same([jnp.concatenate(sums, axis=0)], ones, spread_ref[1], lane8)
     own = jnp.concatenate(
         [jnp.sum(t, axis=0, keepdims=True) for t in tiles] + [jnp.zeros((1, 128), F32)], axis=0
     )
@@ -270,10 +302,7 @@
         lax.fori_loop(max(start, 1), end, take, 0)
         rows = (end - start) * 8
         leaf_lane = lax.broadcasted_iota(jnp.int32, (rows, 128), 1).astype(F32)
-        got = [
-            rbuf[start:end, at : at + 8].reshape(rows, 128) for at in range(0, ROWS, 8)
-        ]
-        for side in (got[0::2], [got[1], got[3], pltpu.roll(got[4], 64, 1)]):
+        for side in unfold(rbuf, start, end):
             hit = jnp.where(side[2][:, 63:64] == leaf_lane, 1.0, 0.0)
             hit = jnp.transpose(hit).astype(BF16)
             high, low = split(jnp.concatenate(side, axis=1))
@@ -321,9 +350,16 @@
 
 def local(devices, low_size, segments, send_counts, send_offsets, leaf_of_block):
     blocks = segments.shape[0]
+    levels = LEAF_DEV.bit_length() - 1 + devices.bit_length() - 1
+    depth = [len(range(d, levels, 3)) for d in range(3)]
+    shift_tiles, tile_places = make_shift_tiles(depth, 2.0 ** (-levels / 2))
+    powers = np.zeros((8, 128), np.int32)
+    powers[:3, :MONOS] = np.array(EXPONENTS).T
     lanes = np.arange(128)
-    one = ((lanes[None, :] % 9 == lanes[:, None] // 8) & (lanes[:, None] < 72)).astype(np.float32)
-    spread = jnp.asarray(np.concatenate([one, one], axis=0), BF16)
+    one = (lanes[None, :] % 9 == lanes[:, None] // 8) & (lanes[:, None] < 72)
+    two = (lanes[None, :] % 9 == lanes[:, None] % 9) & (lanes[:, None] < 126)
+    spread = np.stack([np.concatenate([x, x], axis=0) for x in (one, two)])
+    spread = jnp.asarray(spread.astype(np.float32), BF16)
     perm = jnp.asarray(make_permutation(), BF16)
     hbm = pl.BlockSpec(memory_space=pltpu.HBM)
     dma = pltpu.SemaphoreType.DMA
@@ -332,26 +368,27 @@
         jax.ShapeDtypeStruct((1, COEFFS), F32),
     )
     results = pl.pallas_call(
-        functools.partial(kernel, devices, low_size),
+        functools.partial(kernel, devices, low_size, depth, tile_places),
         out_shape=shapes,
-        in_specs=[hbm] * 6,
+        in_specs=[hbm] * 8,
         out_specs=(hbm, hbm),
         scratch_shapes=[
             pltpu.VMEM((9, blocks + SLOTS, 128), F32),
             pltpu.VMEM((blocks // 128, 128), jnp.int32),
             pltpu.VMEM((320, 384), BF16),
-            pltpu.VMEM((256, 128), BF16),
+            pltpu.VMEM((2, 256, 128), BF16),
             pltpu.SMEM((1, devices), jnp.int32),
             pltpu.SMEM((1, devices), jnp.int32),
-            pltpu.VMEM((4, blocks + SLOTS, 128), F32),
-            pltpu.VMEM((8 * MONOS, 128), F32),
+            pltpu.VMEM(shift_tiles.shape, F32),
+            pltpu.VMEM(powers.shape, jnp.int32),
+            pltpu.VMEM((blocks + SLOTS, 128), F32),
             pltpu.VMEM((devices, ROWS, 128), F32),
             pltpu.VMEM((devices, ROWS, 128), F32),
             pltpu.VMEM((4, 128), F32),
             pltpu.VMEM((devices, 4, 128), F32),
             pltpu.VMEM((COEFFS, LEAF_DEV), F32),
             pltpu.VMEM((1, COEFFS), F32),
-            dma((6,)),
+            dma((8,)),
             dma((devices,)),
             dma((devices,)),
             dma((devices,)),
@@ -371,6 +408,8 @@
         spread,
         send_counts,
         send_offsets,
+        jnp.asarray(shift_tiles),
+        jnp.asarray(powers),
     )
     return pl.pallas_call(
         hand_over,

time: 30.3 us -> 29.9 us (0.987)
  Pallas kernels: 29.5 us -> 29.1 us
    pallas_call x1, Pallas kernels: 27.8 us -> 27.5 us  [local(): pl.pallas_call(functools.partial(kernel, devices, low_size, depth, tile_p...]
where the time goes in v6:
time: 29.9 us; the launch traced here: 29.7 us
  Pallas kernels  29.1 us (97%)
  between operations  0.64 us (2%)
    pallas_call x1, Pallas kernels, local(): pl.pallas_call(functools.partial(kernel, devices, low_size, depth, tile_p...  27.5 us
    pallas_call x1, Pallas kernels, local(): pl.pallas_call(hand_over, out_shape=shapes, in_specs=[hbm, hbm], out_spec...  1.62 us

profile of v6, /device:TPU:0, one launch (start us, length us, event | category | flops | bytes accessed | tf_op | source)
XLA Modules:
  0.0 29.7 jit_solution(7658486192554003293)
XLA Ops:
  0.6 27.5 %shard_map.95 = (f32[315,128]{1,0:T(8,128)}, f32[1,315]{1,0:T(1,128)}) custom-call(f32[9,256,128]{2,1,0:T(8,128)} %bitcast.2, s32[2,128]{1,0:T(2,128)} %bitcast.3, bf16[320,384]{1,0:T(8,128)(2,1)} %constant.9.clone.perm_hbm, bf16[2,256,128]{2,1,0:T(8,128)(2,1)} %constant.8.clone.spread_hbm, s32[1,32]{1,0:T(1,128)} %count_hbm.1, s32[1,32]{1,0:T(1,128)} %offset_hbm.1, ...), custom_call_target="tpu_custom_call" | custom-call | flops 41287680 | bytes 1310720 | tf_op jit(solution)/shard_map/pallas_call | solution.py:370
  28.1 1.6 %shard_map.96 = (f32[315,128]{1,0:T(8,128)}, f32[1,315]{1,0:T(1,128)}) custom-call(f32[315,128]{1,0:T(8,128)} %get-tuple-element.4.leaf_in, f32[1,315]{1,0:T(1,128)} %get-tuple-element.5.root_in), custom_call_target="tpu_custom_call" | custom-call | tf_op jit(solution)/shard_map/pallas_call | solution.py:414

commit v7 on v6

--- a/solution.py
+++ b/solution.py
@@ -107,24 +107,24 @@
     return both[:, :128] + both[:, 128:]
 
 
-def gather_same(products, same, spread, lane):
-    sides = []
-    for one in products:
-        kept = (one.reshape(MONOS, 8, 128) * same).reshape(8 * MONOS, 128)
-        sides.append(jnp.concatenate(split(kept), axis=1))
-    spreaded = dot(jnp.concatenate(sides, axis=0), spread, NN)
-    groups = []
-    for g in range(len(products)):
-        tiles = []
-        for first in (0, 14, 28):
-            count = min(14, MONOS - first)
-            tile = jnp.zeros((8, 128), F32)
-            for k in reversed(range(count)):
-                at = 8 * (MONOS * g + first + k)
-                tile = jnp.where(lane < 9 * k + 9, spreaded[at : at + 8], tile)
-            tiles.append(tile)
-        groups.append(tiles)
-    return groups
+def lay_out(pieces, lane):
+    tiles = []
+    for first in (0, 14, 28):
+        tile = jnp.zeros((8, 128), F32)
+        for k in reversed(range(min(14, MONOS - first))):
+            tile = jnp.where(lane < 9 * k + 9, pieces[first + k], tile)
+        tiles.append(tile)
+    return tiles
+
+
+def pick_same(products, index, lane):
+    pieces = [
+        jnp.take_along_axis(
+            products[8 * m : 8 * m + 8], index, axis=1, mode="promise_in_bounds"
+        )
+        for m in range(MONOS)
+    ]
+    return lay_out(pieces, lane)
 
 
 def column(row):
@@ -187,7 +187,7 @@
 
     lane8 = lax.broadcasted_iota(jnp.int32, (8, 128), 1)
     row8 = lax.broadcasted_iota(jnp.int32, (8, 128), 0)
-    same = jnp.where(lax.rem(lane8, 8) == row8, 1.0, 0.0)
+    same = 8 * lax.rem(lane8, 9) + row8
 
     def load(rows):
         parts = [seg_ref[c, rows, :] for c in range(9)]
@@ -223,7 +223,7 @@
                 leaf = jnp.where(row8 + side < count_ref[0, owner], place[rows, :], -1.0)
                 leaf_rows.append(leaf)
             steps.append(step)
-        made = gather_same(products, same, spread_ref[0], lane8)
+        made = [pick_same(one, same, lane8) for one in products]
         for u, step in enumerate(steps):
             near, far = made[2 * u : 2 * u + 2]
             last_near = jnp.where(lane8 == 63, leaf_rows[2 * u], near[2])
@@ -279,8 +279,9 @@
             term = grown[8 * i : 8 * i + 8, 128 * j : 128 * j + 128] * shift_ref[at]
             total = term if total is None else total + term
         sums.append(total)
-    ones = jnp.ones((8, 128), F32)
-    (tiles,) = gather_same([jnp.concatenate(sums, axis=0)], ones, spread_ref[1], lane8)
+    sums = jnp.concatenate(split(jnp.concatenate(sums, axis=0)), axis=1)
+    sums = dot(sums, spread_ref[...], NN)
+    tiles = lay_out([sums[8 * m : 8 * m + 8] for m in range(MONOS)], lane8)
     own = jnp.concatenate(
         [jnp.sum(t, axis=0, keepdims=True) for t in tiles] + [jnp.zeros((1, 128), F32)], axis=0
     )
@@ -356,10 +357,9 @@
     powers = np.zeros((8, 128), np.int32)
     powers[:3, :MONOS] = np.array(EXPONENTS).T
     lanes = np.arange(128)
-    one = (lanes[None, :] % 9 == lanes[:, None] // 8) & (lanes[:, None] < 72)
-    two = (lanes[None, :] % 9 == lanes[:, None] % 9) & (lanes[:, None] < 126)
-    spread = np.stack([np.concatenate([x, x], axis=0) for x in (one, two)])
-    spread = jnp.asarray(spread.astype(np.float32), BF16)
+    spread = (lanes[None, :] % 9 == lanes[:, None] % 9) & (lanes[:, None] < 126)
+    spread = np.concatenate([spread, spread], axis=0).astype(np.float32)
+    spread = jnp.asarray(spread, BF16)
     perm = jnp.asarray(make_permutation(), BF16)
     hbm = pl.BlockSpec(memory_space=pltpu.HBM)
     dma = pltpu.SemaphoreType.DMA
@@ -376,7 +376,7 @@
             pltpu.VMEM((9, blocks + SLOTS, 128), F32),
             pltpu.VMEM((blocks // 128, 128), jnp.int32),
             pltpu.VMEM((320, 384), BF16),
-            pltpu.VMEM((2, 256, 128), BF16),
+            pltpu.VMEM((256, 128), BF16),
             pltpu.SMEM((1, devices), jnp.int32),
             pltpu.SMEM((1, devices), jnp.int32),
             pltpu.VMEM(shift_tiles.shape, F32),

time: 29.9 us -> 29.7 us (level)
  no operation moved by 1% of the time
where the time goes in v7:
time: 29.7 us; the launch traced here: 29.6 us
  Pallas kernels  28.9 us (97%)
  between operations  0.64 us (2%)
    pallas_call x1, Pallas kernels, local(): pl.pallas_call(functools.partial(kernel, devices, low_size, depth, tile_p...  27.3 us
    pallas_call x1, Pallas kernels, local(): pl.pallas_call(hand_over, out_shape=shapes, in_specs=[hbm, hbm], out_spec...  1.62 us

profile of v7, /device:TPU:0, one launch (start us, length us, event | category | flops | bytes accessed | tf_op | source)
XLA Modules:
  0.0 29.6 jit_solution(2711993076155973384)
XLA Ops:
  0.6 27.3 %shard_map.95 = (f32[315,128]{1,0:T(8,128)}, f32[1,315]{1,0:T(1,128)}) custom-call(f32[9,256,128]{2,1,0:T(8,128)} %bitcast.2, s32[2,128]{1,0:T(2,128)} %bitcast.3, bf16[320,384]{1,0:T(8,128)(2,1)} %constant.9.clone.perm_hbm, bf16[256,128]{1,0:T(8,128)(2,1)} %constant.8.clone.spread_hbm, s32[1,32]{1,0:T(1,128)} %count_hbm.1, s32[1,32]{1,0:T(1,128)} %offset_hbm.1, ...), custom_call_target="tpu_custom_call" | custom-call | flops 41287680 | bytes 1310720 | tf_op jit(solution)/shard_map/pallas_call | solution.py:370
  27.9 1.6 %shard_map.96 = (f32[315,128]{1,0:T(8,128)}, f32[1,315]{1,0:T(1,128)}) custom-call(f32[315,128]{1,0:T(8,128)} %get-tuple-element.4.leaf_in, f32[1,315]{1,0:T(1,128)} %get-tuple-element.5.root_in), custom_call_target="tpu_custom_call" | custom-call | tf_op jit(solution)/shard_map/pallas_call | solution.py:414

commit v8 on v7

--- a/solution.py
+++ b/solution.py
@@ -136,9 +136,9 @@
     seg_hbm, leaf_hbm, perm_hbm, spread_hbm, count_hbm, offset_hbm, shift_hbm, power_hbm,
     leaf_out, root_out,
     seg_ref, leaf_ref, perm_ref, spread_ref, count_ref, offset_ref, shift_ref, power_ref,
-    place, sbuf, rbuf, root_send, root_recv,
+    place, sbuf, rbuf, root_send, top_recv, low_recv,
     leaf_made, root_made,
-    load_sem, send_sem, recv_sem, root_send_sem, root_recv_sem, out_sem,
+    load_sem, send_sem, recv_sem, top_send_sem, top_recv_sem, low_send_sem, low_recv_sem, out_sem,
 ):
     blocks = seg_ref.shape[1] - SLOTS
     body_rows = pl.ds(0, blocks)
@@ -202,12 +202,36 @@
             device_id=partner(step)[1], device_id_type=MESH,
         )
 
-    def root_copy(step):
+    my_top, my_low = lax.axis_index("top"), lax.axis_index("low")
+    top_size = devices // low_size
+
+    def top_copy(step):
         return pltpu.make_async_remote_copy(
-            src_ref=root_send, dst_ref=root_recv.at[step],
-            send_sem=root_send_sem.at[step], recv_sem=root_recv_sem.at[step],
-            device_id=partner(step)[1], device_id_type=MESH,
-        )
+            src_ref=root_send.at[0], dst_ref=top_recv.at[step],
+            send_sem=top_send_sem.at[step], recv_sem=top_recv_sem.at[step],
+            device_id=(lax.rem(my_top + step, top_size), my_low), device_id_type=MESH,
+        )
+
+    def low_copy(step):
+        return pltpu.make_async_remote_copy(
+            src_ref=root_send.at[1], dst_ref=low_recv.at[step],
+            send_sem=low_send_sem.at[step], recv_sem=low_recv_sem.at[step],
+            device_id=(my_top, lax.rem(my_low + step, low_size)), device_id_type=MESH,
+        )
+
+    def start_all(copy, count):
+        def body(step, carry):
+            copy(step).start()
+            return carry
+
+        lax.fori_loop(1, count, body, 0)
+
+    def wait_all(copy, count):
+        def body(step, carry):
+            copy(step).wait()
+            return carry
+
+        lax.fori_loop(1, count, body, 0)
 
     pl.semaphore_wait(barrier, devices - 1)
 
@@ -285,22 +309,22 @@
     own = jnp.concatenate(
         [jnp.sum(t, axis=0, keepdims=True) for t in tiles] + [jnp.zeros((1, 128), F32)], axis=0
     )
-    root_send[...] = own
-
-    def send_root(step, carry):
-        root_copy(step).start()
-        return carry
-
-    lax.fori_loop(1, devices, send_root, 0)
+    root_send[0] = own
+    start_all(top_copy, top_size)
 
     def take(step, carry):
         block_copy(step).wait()
         return carry
 
     cells = jnp.zeros((LEAF_DEV, 384), F32)
-    bounds = [0, devices // 2, devices // 8 * 7, devices]
+    bounds = [0, devices // 2, devices // 4 * 3, devices // 8 * 7, devices]
     for start, end in zip(bounds[:-1], bounds[1:]):
         lax.fori_loop(max(start, 1), end, take, 0)
+        if end == bounds[2]:
+            wait_all(top_copy, top_size)
+            top_recv[0] = own
+            root_send[1] = jnp.sum(top_recv[...], axis=0)
+            start_all(low_copy, low_size)
         rows = (end - start) * 8
         leaf_lane = lax.broadcasted_iota(jnp.int32, (rows, 128), 1).astype(F32)
         for side in unfold(rbuf, start, end):
@@ -315,13 +339,9 @@
     leaf_store = pltpu.make_async_copy(leaf_made, leaf_out, out_sem.at[0])
     leaf_store.start()
 
-    def take_root(step, carry):
-        root_copy(step).wait()
-        return carry
-
-    lax.fori_loop(1, devices, take_root, 0)
-    root_recv[0] = own
-    total = jnp.sum(root_recv[...], axis=0)
+    wait_all(low_copy, low_size)
+    low_recv[0] = root_send[1]
+    total = jnp.sum(low_recv[...], axis=0)
     line = jnp.concatenate([total[0:1], total[1:2], total[2:3]], axis=1)
     high, low = split(jnp.broadcast_to(line, (16, 384)))
     root_made[...] = (dot(high, perm, NT) + dot(low, perm, NT))[0:1, :COEFFS]
@@ -384,15 +404,18 @@
             pltpu.VMEM((blocks + SLOTS, 128), F32),
             pltpu.VMEM((devices, ROWS, 128), F32),
             pltpu.VMEM((devices, ROWS, 128), F32),
-            pltpu.VMEM((4, 128), F32),
-            pltpu.VMEM((devices, 4, 128), F32),
+            pltpu.VMEM((2, 4, 128), F32),
+            pltpu.VMEM((devices // low_size, 4, 128), F32),
+            pltpu.VMEM((low_size, 4, 128), F32),
             pltpu.VMEM((COEFFS, LEAF_DEV), F32),
             pltpu.VMEM((1, COEFFS), F32),
             dma((8,)),
             dma((devices,)),
             dma((devices,)),
-            dma((devices,)),
-            dma((devices,)),
+            dma((devices // low_size,)),
+            dma((devices // low_size,)),
+            dma((low_size,)),
+            dma((low_size,)),
             dma((2,)),
         ],
         compiler_params=pltpu.CompilerParams(

time: 29.7 us -> 31.3 us (1.054)
  Pallas kernels: 28.9 us -> 30.5 us
    pallas_call x1, Pallas kernels: 27.3 us -> 28.9 us  [local(): pl.pallas_call(functools.partial(kernel, devices, low_size, depth, tile_p...]
where the time goes in v8:
time: 31.3 us; the launch traced here: 31.1 us
  Pallas kernels  30.5 us (97%)
  between operations  0.64 us (2%)
    pallas_call x1, Pallas kernels, local(): pl.pallas_call(functools.partial(kernel, devices, low_size, depth, tile_p...  28.9 us
    pallas_call x1, Pallas kernels, local(): pl.pallas_call(hand_over, out_shape=shapes, in_specs=[hbm, hbm], out_spec...  1.62 us

profile of v8, /device:TPU:0, one launch (start us, length us, event | category | flops | bytes accessed | tf_op | source)
XLA Modules:
  0.0 31.1 jit_solution(4301958189328908750)
XLA Ops:
  0.6 28.9 %shard_map.95 = (f32[315,128]{1,0:T(8,128)}, f32[1,315]{1,0:T(1,128)}) custom-call(f32[9,256,128]{2,1,0:T(8,128)} %bitcast.2, s32[2,128]{1,0:T(2,128)} %bitcast.3, bf16[320,384]{1,0:T(8,128)(2,1)} %constant.9.clone.perm_hbm, bf16[256,128]{1,0:T(8,128)(2,1)} %constant.8.clone.spread_hbm, s32[1,32]{1,0:T(1,128)} %count_hbm.1, s32[1,32]{1,0:T(1,128)} %offset_hbm.1, ...), custom_call_target="tpu_custom_call" | custom-call | flops 41287680 | bytes 1310720 | tf_op jit(solution)/shard_map/pallas_call | solution.py:390
  29.5 1.6 %shard_map.96 = (f32[315,128]{1,0:T(8,128)}, f32[1,315]{1,0:T(1,128)}) custom-call(f32[315,128]{1,0:T(8,128)} %get-tuple-element.4.leaf_in, f32[1,315]{1,0:T(1,128)} %get-tuple-element.5.root_in), custom_call_target="tpu_custom_call" | custom-call | tf_op jit(solution)/shard_map/pallas_call | solution.py:437

commit v9 on v7

--- a/solution.py
+++ b/solution.py
@@ -162,8 +162,12 @@
 
     me = lax.axis_index("top") * low_size + lax.axis_index("low")
 
+    def distance(step):
+        later = jnp.where(step + 3 >= devices, step + 4 - devices, step + 3)
+        return jnp.where(step == 0, 0, later)
+
     def partner(step):
-        other = lax.rem(me + step, devices)
+        other = lax.rem(me + distance(step), devices)
         return other, (other // low_size, lax.rem(other, low_size))
 
     barrier = pltpu.get_barrier_semaphore()
@@ -252,7 +256,8 @@
     fetches[7].wait()
     rows = devices * 8
     shape = (rows, 128)
-    owner = me + lax.shift_right_logical(lax.broadcasted_iota(jnp.int32, shape, 0), 3)
+    steps = lax.shift_right_logical(lax.broadcasted_iota(jnp.int32, shape, 0), 3)
+    owner = me + distance(steps)
     owner = jnp.where(owner >= devices, owner - devices, owner)
     powers = [power_ref[d : d + 1, :] for d in range(3)]
     lane_used = lax.broadcasted_iota(jnp.int32, shape, 1) < MONOS

time: 29.7 us -> 29.7 us (level)
  no operation moved by 1% of the time
where the time goes in v9:
time: 29.7 us; the launch traced here: 29.6 us
  Pallas kernels  28.9 us (97%)
  between operations  0.64 us (2%)
    pallas_call x1, Pallas kernels, local(): pl.pallas_call(functools.partial(kernel, devices, low_size, depth, tile_p...  27.3 us
    pallas_call x1, Pallas kernels, local(): pl.pallas_call(hand_over, out_shape=shapes, in_specs=[hbm, hbm], out_spec...  1.62 us

profile of v9, /device:TPU:0, one launch (start us, length us, event | category | flops | bytes accessed | tf_op | source)
XLA Modules:
  0.0 29.6 jit_solution(9203236628820562643)
XLA Ops:
  0.6 27.3 %shard_map.95 = (f32[315,128]{1,0:T(8,128)}, f32[1,315]{1,0:T(1,128)}) custom-call(f32[9,256,128]{2,1,0:T(8,128)} %bitcast.2, s32[2,128]{1,0:T(2,128)} %bitcast.3, bf16[320,384]{1,0:T(8,128)(2,1)} %constant.9.clone.perm_hbm, bf16[256,128]{1,0:T(8,128)(2,1)} %constant.8.clone.spread_hbm, s32[1,32]{1,0:T(1,128)} %count_hbm.1, s32[1,32]{1,0:T(1,128)} %offset_hbm.1, ...), custom_call_target="tpu_custom_call" | custom-call | flops 41287680 | bytes 1310720 | tf_op jit(solution)/shard_map/pallas_call | solution.py:375
  27.9 1.6 %shard_map.96 = (f32[315,128]{1,0:T(8,128)}, f32[1,315]{1,0:T(1,128)}) custom-call(f32[315,128]{1,0:T(8,128)} %get-tuple-element.4.leaf_in, f32[1,315]{1,0:T(1,128)} %get-tuple-element.5.root_in), custom_call_target="tpu_custom_call" | custom-call | tf_op jit(solution)/shard_map/pallas_call | solution.py:419
